TPU v7x, 512 devices: a whole 4x4x16 slice. The times are simulated.
512 devices in a mesh: src: 32 (over x, y, core), tgt: 16 (over z).
Axes of the slice: x: 4, y: 4, z: 16, core: 2. Of those that a mesh axis runs over, the one named last changes fastest.
Arguments:
- sources: float32 [65536, 128], P('src'), may hold values from -3 to 3
- targets: float32 [16384, 128], P('tgt'), may hold values from -3 to 3
- log_source: float32 [65536], P('src'), may hold values from -1 to 1
- log_target: float32 [16384], P('tgt'), may hold values from -1 to 1
Outputs:
- source_potential: float32 [65536], P('src')
- target_potential: float32 [16384], P('tgt')
- barycentric: float32 [65536, 128], P('src')
All inputs are finite; a program needn't handle non-finite values.
Results may differ from a plain program's by a relative error of at most 0.0003.
Values sent between devices are 32-bit elements; how exact they have to be, the bound alone decides.
A program may use at most 64 MiB of HBM per device.

v0:
```python
import jax
import jax.numpy as jnp
from jax import lax
from jax.sharding import PartitionSpec as P

ITERS = 2


EPSILON = 1.0


def row_lse(scores):
    top_score = lax.pmax(jnp.max(scores, axis=1), "tgt")
    exp_total = lax.psum(jnp.sum(jnp.exp(scores - top_score[:, None]), axis=1), "tgt")
    return top_score + jnp.log(exp_total)


def column_lse(scores):
    top_score = lax.pmax(jnp.max(scores, axis=0), "src")
    exp_total = lax.psum(jnp.sum(jnp.exp(scores - top_score[None, :]), axis=0), "src")
    return top_score + jnp.log(exp_total)


def on_device(sources, targets, log_source, log_target):
    src_norms = jnp.sum(sources * sources, axis=1)
    tgt_norms = jnp.sum(targets * targets, axis=1)

    def build_tile():
        inner = jnp.dot(
            sources, targets.T, precision=lax.Precision.HIGHEST, preferred_element_type=jnp.float32
        )
        return src_norms[:, None] + tgt_norms[None, :] - 2.0 * inner

    def cost_tile():
        return build_tile()

    target_pot = jnp.zeros((targets.shape[0],), jnp.float32)
    source_pot = jnp.zeros((sources.shape[0],), jnp.float32)
    for repeat in range(ITERS):
        scores = (target_pot[None, :] - cost_tile()) / EPSILON
        source_pot = EPSILON * log_source - EPSILON * row_lse(scores)
        scores = (source_pot[:, None] - cost_tile()) / EPSILON
        target_pot = EPSILON * log_target - EPSILON * column_lse(scores)
    scores = (target_pot[None, :] - cost_tile()) / EPSILON
    top_score = lax.pmax(jnp.max(scores, axis=1), "tgt")
    weights = jnp.exp(scores - top_score[:, None])
    weight_sum = jnp.sum(weights, axis=1)
    weighted = jnp.dot(
        weights, targets, precision=lax.Precision.HIGHEST, preferred_element_type=jnp.float32
    )
    total_sum, total_weighted = lax.psum((weight_sum, weighted), "tgt")
    barycentric = total_weighted / total_sum[:, None]
    return (source_pot, target_pot, barycentric)


def solution(mesh):
    in_specs = (P("src", None), P("tgt", None), P("src"), P("tgt"))
    out_specs = (P("src"), P("tgt"), P("src", None))
    return jax.shard_map(
        on_device, mesh=mesh, in_specs=in_specs, out_specs=out_specs, check_vma=False
    )
```

profile of v0, /device:TPU:6, one launch (start us, length us, event | category | flops | bytes accessed | tf_op | source)
XLA Modules:
  0.0 613.7 jit_solution(13729030816704503533)
XLA Ops:
  8.5 1.6 multiply_reduce_fusion
  10.0 11.0 %subtract_reduce_fusion.4 = (f32[2048]{0:T(1024)S(1)}, f32[2048,1024]{0,1:T(8,128)}) fusion(f32[2048,128]{1,0:T(8,128)} %param.4, f32[1024,128]{1,0:T(8,128)} %param.5, f32[1024]{0:T(1024)S(1)} %multiply_reduce_fusion.1, f32[2048]{0:T(1024)S(1)} %multiply_reduce_fusion), kind=kOutput, calls=%fused_computation.10 | convolution fusion | flops 3231709184 | bytes 9981952 | tf_op jit(solution)/shard_map/dot_general | solution.py:29
  21.0 37.0 %pmax.35 = f32[2048]{0:T(1024)S(1)} all-reduce(f32[2048]{0:T(1024)S(1)} %get-tuple-element.3), channel_id=1, replica_groups=mesh['src'=32,'tgt'=16] {'tgt'}, use_global_device_ids=true, to_apply=%region_3.0 | all-reduce | flops 2048 | bytes 16384 | tf_op jit(solution)/shard_map/pmax | solution.py:13
  58.0 4.8 exponential_reduce_fusion.3
  62.8 27.5 %psum.42 = f32[2048]{0:T(1024)S(1)} all-reduce(f32[2048]{0:T(1024)S(1)} %exponential_reduce_fusion.3), channel_id=1, replica_groups=mesh['src'=32,'tgt'=16] {'tgt'}, use_global_device_ids=true, to_apply=%region_5.0 | all-reduce | flops 2048 | bytes 16384 | tf_op jit(solution)/shard_map/psum | solution.py:14
  90.4 4.0 subtract_reduce_fusion.3
  94.4 53.0 %pmax.36 = f32[1024]{0:T(1024)S(1)} all-reduce(f32[1024]{0:T(1024)S(1)} %subtract_reduce_fusion.3), channel_id=1, replica_groups=mesh['src'=32,'tgt'=16] {'src'}, use_global_device_ids=true, to_apply=%region_7.0 | all-reduce | flops 1024 | bytes 8192 | tf_op jit(solution)/shard_map/pmax | solution.py:19
  147.4 4.4 exponential_reduce_fusion.2
  151.8 54.4 %psum.43 = f32[1024]{0:T(1024)S(1)} all-reduce(f32[1024]{0:T(1024)S(1)} %exponential_reduce_fusion.2), channel_id=1, replica_groups=mesh['src'=32,'tgt'=16] {'src'}, use_global_device_ids=true, to_apply=%region_9.0 | all-reduce | flops 1024 | bytes 8192 | tf_op jit(solution)/shard_map/psum | solution.py:20
  206.2 4.0 subtract_reduce_fusion.2
  210.2 29.5 %pmax.37 = f32[2048]{0:T(1024)S(1)} all-reduce(f32[2048]{0:T(1024)S(1)} %subtract_reduce_fusion.2), channel_id=1, replica_groups=mesh['src'=32,'tgt'=16] {'tgt'}, use_global_device_ids=true, to_apply=%region_11.0 | all-reduce | flops 2048 | bytes 16384 | tf_op jit(solution)/shard_map/pmax | solution.py:13
  239.7 4.3 exponential_reduce_fusion.1
  244.1 27.5 %psum.44 = f32[2048]{0:T(1024)S(1)} all-reduce(f32[2048]{0:T(1024)S(1)} %exponential_reduce_fusion.1), channel_id=1, replica_groups=mesh['src'=32,'tgt'=16] {'tgt'}, use_global_device_ids=true, to_apply=%region_13.0 | all-reduce | flops 2048 | bytes 16384 | tf_op jit(solution)/shard_map/psum | solution.py:14
  271.6 4.0 subtract_reduce_fusion.1
  275.6 62.8 %pmax.38 = f32[1024]{0:T(1024)S(1)} all-reduce(f32[1024]{0:T(1024)S(1)} %subtract_reduce_fusion.1), channel_id=1, replica_groups=mesh['src'=32,'tgt'=16] {'src'}, use_global_device_ids=true, to_apply=%region_15.0 | all-reduce | flops 1024 | bytes 8192 | tf_op jit(solution)/shard_map/pmax | solution.py:19
  338.5 4.4 exponential_reduce_fusion
  342.9 62.8 %psum.45 = f32[1024]{0:T(1024)S(1)} all-reduce(f32[1024]{0:T(1024)S(1)} %exponential_reduce_fusion), channel_id=1, replica_groups=mesh['src'=32,'tgt'=16] {'src'}, use_global_device_ids=true, to_apply=%region_17.0 | all-reduce | flops 1024 | bytes 8192 | tf_op jit(solution)/shard_map/psum | solution.py:20
  405.8 4.0 subtract_reduce_fusion
  409.8 29.5 %pmax.39 = f32[2048]{0:T(1024)S(1)} all-reduce(f32[2048]{0:T(1024)S(1)} %subtract_reduce_fusion), channel_id=1, replica_groups=mesh['src'=32,'tgt'=16] {'tgt'}, use_global_device_ids=true, to_apply=%region_19.0 | all-reduce | flops 2048 | bytes 16384 | tf_op jit(solution)/shard_map/pmax | solution.py:45
  439.3 16.9 %fusion.1 = f32[2048,128]{1,0:T(8,128)} fusion(f32[1024,128]{1,0:T(8,128)S(1)} %copy-done, f32[2048,1024]{0,1:T(8,128)} %get-tuple-element.4, f32[2048]{0:T(1024)S(1)} %pmax.39, f32[1024]{0:T(1024)S(1)} %add_subtract_fusion.2), kind=kOutput, calls=%fused_computation.12 | convolution fusion | flops 3225419776 | bytes 9973760 | tf_op jit(solution)/shard_map/dot_general | solution.py:48
  456.3 4.3 fusion
  460.6 27.6 %psum.47 = f32[2048]{0:T(1024)S(1)} all-reduce(f32[2048]{0:T(1024)S(1)} %fusion), channel_id=1, replica_groups=mesh['src'=32,'tgt'=16] {'tgt'}, use_global_device_ids=true, to_apply=%region_22.0 | all-reduce | flops 2048 | bytes 16384 | tf_op jit(solution)/shard_map/psum | solution.py:51
  488.2 116.1 %all-reduce.2.cloned.1.call-done = f32[2048,128]{1,0:T(8,128)} async-done(((f32[2048,128]{1,0:T(8,128)}), f32[2048,128]{1,0:T(8,128)}) %all-reduce.2.cloned.1.call-update) | async-done | bytes 1048592 | tf_op jit(solution)/shard_map/psum | solution.py:51
  604.3 2.5 broadcast_divide_fusion
  (17 shorter events, 1.4 us)
Async XLA Ops:
  7.2 597.1 %all-reduce.2.cloned.1.call-start = ((), (), s32[]{:S(2)}) async-start(), calls=%async_computation | async-start | bytes 2097152 | tf_op jit(solution)/shard_map/psum | solution.py:51
  21.0 69.3 %copy-start.3 = (f32[2048]{0:T(1024)S(1)}, f32[2048]{0:T(1024)}, u32[]{:S(2)}) copy-start(f32[2048]{0:T(1024)} %param.6) | copy-start | bytes 24580
  90.4 115.8 %copy-start.4 = (f32[1024]{0:T(1024)S(1)}, f32[1024]{0:T(1024)}, u32[]{:S(2)}) copy-start(f32[1024]{0:T(1024)} %param.7) | copy-start | bytes 12292
  271.6 71.3 %copy-start.1 = (f32[2048]{0:T(1024)}, f32[2048]{0:T(1024)S(1)}, u32[]{:S(2)}) copy-start(f32[2048]{0:T(1024)S(1)} %add_subtract_fusion) | copy-start | bytes 24580
  338.5 100.8 %copy-start = (f32[1024,128]{1,0:T(8,128)S(1)}, f32[1024,128]{1,0:T(8,128)}, u32[]{:S(2)}) copy-start(f32[1024,128]{1,0:T(8,128)} %param.5) | copy-start | bytes 1572868
  405.7 50.5 %copy-start.2 = (f32[1024]{0:T(1024)}, f32[1024]{0:T(1024)S(1)}, u32[]{:S(2)}) copy-start(f32[1024]{0:T(1024)S(1)} %add_subtract_fusion.2) | copy-start | bytes 12292
Sparse Core Ops, SparseCore 0:
  456.4 147.8 all-reduce.1
where the time goes:
time: 614 us
  blocking collectives  412 us (67%)
  waiting for transfers between devices  116 us (19%)
  other arithmetic  43.6 us (7%)
  matrix products  27.9 us (5%)
  between operations  14.2 us (2%)
    psum x2, blocking collectives, column_lse(): lax.psum(jnp.sum(jnp.exp(scores - top_score[None, :]), axis=0), 'src')  117 us
    psum x1, waiting for transfers between devices, on_device(): total_sum, total_weighted = lax.psum((weight_sum, weighted), 'tgt')  116 us
    pmax x2, blocking collectives, column_lse(): top_score = lax.pmax(jnp.max(scores, axis=0), 'src')  116 us
    pmax x2, blocking collectives, row_lse(): top_score = lax.pmax(jnp.max(scores, axis=1), 'tgt')  66.5 us
    psum x2, blocking collectives, row_lse(): lax.psum(jnp.sum(jnp.exp(scores - top_score[:, None]), axis=1), 'tgt')  55.1 us
    pmax x1, blocking collectives, on_device(): top_score = lax.pmax(jnp.max(scores, axis=1), 'tgt')  29.5 us
    psum x1, blocking collectives, on_device(): total_sum, total_weighted = lax.psum((weight_sum, weighted), 'tgt')  27.6 us
    dot_general x1, matrix products, on_device(): jnp.dot(weights, targets, precision=lax.Precision.HIGHEST, preferred_elem...  16.9 us
  transfers between devices with their start and end apart: 1, of which 1 were waited for; matrix products, arithmetic and copies ran while one was open for 1% of the time, Pallas kernels for 0%

commit v1 on v0

v1 whole, which is shorter than its diff:
```python
import math

import jax
import jax.numpy as jnp
from jax import lax
from jax.experimental import pallas as pl
from jax.experimental.pallas import tpu as pltpu
from jax.sharding import PartitionSpec as P

ITERS = 2
LATENT = 128
LANES = 128
LOG2E = math.log2(math.e)
LN2 = math.log(2.0)
MESH = pl.DeviceIdType.MESH

NSRC, NTGT = 32, 16
GRID_X, GRID_Y = 4, 4
ROWS, COLS = 2048, 1024
RCH, CCH = ROWS // LANES, COLS // LANES
OWN = ROWS // NTGT
HALF = COLS // 2
PIECE = HALF // 8
F32, BF16 = jnp.float32, jnp.bfloat16


def split3(v, order):
    high = v.astype(BF16)
    low = (v - high.astype(F32)).astype(BF16)
    return jnp.concatenate([(high, low)[k] for k in order], axis=1)


def nt_dot(a, b):
    return lax.dot_general(a, b, (((1,), (1,)), ((), ())), preferred_element_type=F32)


def spread(row):
    return jnp.broadcast_to(row, (LANES, LANES)).T


def lse_pass(z_ref, b_ref, rows, cols, put):
    width, depth = 4, 64

    def load(block, col, k):
        at = pl.ds(pl.multiple_of(block * depth, depth), depth)
        lane = pl.multiple_of(col * width * LANES + k * LANES, LANES)
        return (z_ref[at, pl.ds(lane, LANES)] + b_ref[at, :]).reshape(depth // 8, 8, LANES)

    @pl.loop(0, cols // (width * LANES))
    def _(col):
        def top(block, acc):
            return tuple(jnp.maximum(acc[k], jnp.max(load(block, col, k), axis=0)) for k in range(width))

        start = tuple(jnp.full((8, LANES), -jnp.inf, F32) for _ in range(width))
        tops = lax.fori_loop(0, rows // depth, top, start)
        tops = [jnp.max(v, axis=0, keepdims=True) for v in tops]

        def total(block, acc):
            return tuple(
                acc[k] + jnp.sum(jnp.exp2(load(block, col, k) - tops[k].reshape(1, 1, LANES)), axis=0)
                for k in range(width)
            )

        sums = lax.fori_loop(0, rows // depth, total, tuple(jnp.zeros((8, LANES), F32) for _ in range(width)))
        for k in range(width):
            put(col * width + k, tops[k] + LOG2E * jnp.log(jnp.sum(sums[k], axis=0, keepdims=True)))


def combine(parts):
    top = jnp.max(parts, axis=0)
    return top + LOG2E * jnp.log(jnp.sum(jnp.exp2(parts - top[None]), axis=0))


def kernel(
    x_ref, y_ref, la_ref, lb_ref, sp_ref, tp_ref, out_ref,
    xa, ya, zt, z, qb, pb, nx, ny,
    l_row, rs, pg, l_col, cr, qs, qg, tg, xs, yf, zf, mf, sf, acc, part, sib,
    rs_send, rs_recv, pg_send, pg_recv, cr_send, cr_recv, qg_send, qg_recv,
    tr_send, tr_recv, plane_send, plane_recv, or_send, or_recv, xs_sem, sib_sem,
):
    s, t = lax.axis_index("src"), lax.axis_index("tgt")
    gx, gy, core = s // (GRID_Y * 2), lax.rem(s // 2, GRID_Y), lax.rem(s, 2)
    mate = s + 1 - 2 * core

    def z_peer(k):
        return lax.rem(t + k, NTGT)

    def s_peer(k):
        return lax.rem(s + k, NSRC)

    barrier = pltpu.get_barrier_semaphore()

    @pl.loop(1, NTGT)
    def _(k):
        pl.semaphore_signal(barrier, inc=1, device_id=(s, z_peer(k)), device_id_type=MESH)

    @pl.loop(1, NSRC)
    def _(k):
        pl.semaphore_signal(barrier, inc=1, device_id=(s_peer(k), t), device_id_type=MESH)

    def remote(src, dst, send, recv, device):
        return pltpu.make_async_remote_copy(
            src_ref=src, dst_ref=dst, send_sem=send, recv_sem=recv, device_id=device, device_id_type=MESH
        )

    @pl.loop(0, ROWS // 256)
    def _(k):
        at = pl.ds(pl.multiple_of(k * 256, 256), 256)
        xa[at, :] = split3(x_ref[at, :] * (2.0 * LOG2E), (0, 0, 1))

    @pl.loop(0, COLS // 256)
    def _(k):
        at = pl.ds(pl.multiple_of(k * 256, 256), 256)
        y = y_ref[at, :]
        ya[at, :] = split3(y, (0, 1, 0))
        qb[at, :] = jnp.broadcast_to(-LOG2E * jnp.sum(y * y, axis=1, keepdims=True), (256, LANES))

    slots = (gx, GRID_X + gy)
    for slot in slots:
        tg[slot, t] = y_ref[pl.ds(pl.multiple_of(core * HALF + slot * PIECE, PIECE), PIECE), :]
    own_rows = pl.ds(pl.multiple_of(t * OWN, OWN), OWN)
    xs[core] = x_ref[own_rows, :]

    pl.semaphore_wait(barrier, NTGT - 1 + NSRC - 1)

    def hops(way, chunk):
        return NTGT // 2 - (way ^ chunk)

    def ring_copy(view, send, recv, way, chunk, step):
        block = lax.rem(t + NTGT - step, NTGT) if way == 0 else lax.rem(t + step, NTGT)
        to = lax.rem(t + 1, NTGT) if way == 0 else lax.rem(t + NTGT - 1, NTGT)
        ref = view(chunk, block)
        return remote(ref, ref, send.at[way, chunk, step], recv.at[way, chunk, step], (s, to)), block

    def ring_arrival(view, send, recv, way, chunk, step):
        block = lax.rem(t + NTGT - step, NTGT) if way == 0 else lax.rem(t + step, NTGT)
        ref = view(chunk, block)
        remote(ref, ref, send.at[way, chunk, step - 1], recv.at[way, chunk, step - 1], (s, t)).wait_recv()
        return block

    def ring_step(view, send, recv, step, then=None):
        for chunk in range(2):
            for way in range(2):
                if step > hops(way, chunk):
                    continue
                block = t
                if step > 0:
                    block = ring_arrival(view, send, recv, way, chunk, step)
                if step < hops(way, chunk):
                    ring_copy(view, send, recv, way, chunk, step)[0].start()
                if then is not None and (step > 0 or way == 0):
                    then(chunk, block)

    def ring_drain(view, send, recv):
        for chunk in range(2):
            for way in range(2):
                for step in range(hops(way, chunk)):
                    ring_copy(view, send, recv, way, chunk, step)[0].wait_send()

    def plane_peer(chunk, k):
        if chunk == 0:
            return lax.rem(s + k * GRID_Y * 2, NSRC)
        return (gx * GRID_Y + lax.rem(gy + k, GRID_Y)) * 2 + core

    def plane_copy(chunk, k, ref):
        return remote(
            ref, ref, plane_send.at[chunk, k - 1], plane_recv.at[slots[chunk]], (plane_peer(chunk, k), t)
        )

    def to_plane(chunk, block):
        for k in range(1, 4):
            plane_copy(chunk, k, tg.at[slots[chunk], block]).start()

    def t_view(chunk, block):
        return tg.at[slots[chunk], block]

    def t_step(step):
        ring_step(t_view, tr_send, tr_recv, step, to_plane)

    def xs_copy():
        return remote(xs.at[core], xs.at[core], xs_sem.at[0], xs_sem.at[1], (mate, t))

    t_step(0)
    xs_copy().start()

    @pl.loop(0, ROWS // 256)
    def _(k):
        at = pl.ds(pl.multiple_of(k * 256, 256), 256)
        zt[:, at] = nt_dot(ya[...], xa[at, :])

    t_step(1)

    def row_copy(it, k):
        to = z_peer(k)
        return remote(l_row.at[it, to], rs.at[it, t], rs_send.at[it, to], rs_recv.at[it, t], (s, to))

    def pot_copy(it, k):
        to = z_peer(k)
        return remote(pg.at[it, t], pg.at[it, t], pg_send.at[it, to], pg_recv.at[it, t], (s, to))

    def col_copy(it, k):
        to = s_peer(k)
        return remote(l_col.at[it], cr.at[it, s], cr_send.at[it, to], cr_recv.at[it, s], (to, t))

    def last_copy(k):
        to = z_peer(k)
        return remote(qs.at[core], qg.at[t], qg_send.at[to], qg_recv.at[t], (s, to))

    for it in range(ITERS):

        def put_row(chunk, value):
            l_row[it, chunk] = value

        lse_pass(zt, qb, COLS, ROWS, put_row)
        rs[it, t] = l_row[it, t]

        @pl.loop(1, NTGT)
        def _(k):
            row_copy(it, k).start()

        if it == 0:
            t_step(2)
            for half in range(2):
                @pl.loop(half * 2, half * 2 + 2)
                def _(k):
                    at = pl.ds(pl.multiple_of(k * 256, 256), 256)
                    z[:, at] = nt_dot(xa[...], ya[at, :])

                if half == 0:
                    t_step(3)
        else:
            t_step(7)

        @pl.loop(1, NTGT)
        def _(k):
            frm = z_peer(k)
            remote(l_row.at[it, frm], rs.at[it, frm], rs_send.at[it, frm], rs_recv.at[it, frm], (s, frm)).wait_recv()

        pg[it, t] = LOG2E * la_ref[t] - combine(rs[it])

        @pl.loop(1, NTGT)
        def _(k):
            pot_copy(it, k).start()

        if it == 0:
            t_step(4)

            @pl.loop(0, RCH)
            def _(k):
                block = x_ref[pl.ds(pl.multiple_of(k * LANES, LANES), LANES), :]
                nx[k] = jnp.sum((block * block).T, axis=0, keepdims=True)

            for k in range(CCH):
                ny[k : k + 1, :] = qb[k * LANES : (k + 1) * LANES, :].T[0:1, :] * (-LN2)
        else:
            t_step(8)

        @pl.loop(1, NTGT)
        def _(k):
            frm = z_peer(k)
            remote(pg.at[it, frm], pg.at[it, frm], pg_send.at[it, frm], pg_recv.at[it, frm], (s, frm)).wait_recv()

        @pl.loop(0, RCH)
        def _(k):
            pb[pl.ds(pl.multiple_of(k * LANES, LANES), LANES), :] = spread(pg[it, k])

        def put_col(chunk, value):
            l_col[it, pl.ds(chunk, 1), :] = value

        lse_pass(z, pb, ROWS, COLS, put_col)

        @pl.loop(1, NSRC)
        def _(k):
            col_copy(it, k).start()

        cr[it, s] = l_col[it]
        if it == 0:
            t_step(5)
        else:
            sp_ref[...] = pg[it] * LN2 + nx[...]
            for slot in range(8):
                chunk, place = slot // 4, slot % 4

                @pl.when(slot != slots[chunk])
                def _():
                    remote(
                        tg.at[slot], tg.at[slot], plane_send.at[chunk, 0], plane_recv.at[slot], (s, t)
                    ).wait_recv()

            xs_mine = xs.at[1 - core]
            remote(xs_mine, xs_mine, xs_sem.at[0], xs_sem.at[1], (mate, t)).wait_recv()
            xf = split3(xs[...].reshape(2 * OWN, LATENT) * (2.0 * LOG2E), (0, 0, 1))
            xa[0 : 2 * OWN, :] = xf

            @pl.loop(0, NTGT)
            def _(b):
                at = pl.ds(pl.multiple_of(b * HALF, HALF), HALF)
                yf[at, :] = split3(tg[:, b].reshape(HALF, LATENT), (0, 1, 0))
                zf[:, at] = nt_dot(xa[0 : 2 * OWN, :], yf[at, :])

        @pl.loop(1, NSRC)
        def _(k):
            frm = s_peer(k)
            remote(l_col.at[it], cr.at[it, frm], cr_send.at[it, frm], cr_recv.at[it, frm], (frm, t)).wait_recv()

        q = LOG2E * lb_ref[...] - combine(cr[it])
        if it == 0:
            for k in range(CCH):
                qb[k * LANES : (k + 1) * LANES, :] = spread(q[k : k + 1, :])
            t_step(6)

    qs[0] = q[0 : CCH // 2, :]
    qs[1] = q[CCH // 2 :, :]
    qg[t] = qs[core]

    @pl.loop(1, NTGT)
    def _(k):
        last_copy(k).start()

    tp_ref[...] = q * LN2 + ny[...]

    @pl.loop(1, NTGT)
    def _(k):
        frm = z_peer(k)
        remote(qs.at[core], qg.at[frm], qg_send.at[frm], qg_recv.at[frm], (s, frm)).wait_recv()

    depth = 64

    @pl.loop(0, 2 * OWN // depth)
    def _(r):
        at = pl.ds(pl.multiple_of(r * depth, depth), depth)

        def top(b, best):
            for k in range(HALF // LANES):
                lane = pl.ds(pl.multiple_of(b * HALF + k * LANES, LANES), LANES)
                best = jnp.maximum(best, zf[at, lane] + qg[b, k : k + 1, :])
            return best

        best = lax.fori_loop(0, NTGT, top, jnp.full((depth, LANES), -jnp.inf, F32))
        mf[at, :] = jnp.broadcast_to(jnp.max(best, axis=1, keepdims=True), (depth, LANES))

    sf[...] = jnp.zeros_like(sf)
    acc[...] = jnp.zeros_like(acc)

    @pl.loop(0, NTGT)
    def _(b):
        highs, lows = [], []
        total = sf[...]
        for k in range(HALF // LANES):
            lane = pl.ds(pl.multiple_of(b * HALF + k * LANES, LANES), LANES)
            w = jnp.exp2(zf[:, lane] + qg[b, k : k + 1, :] - mf[...])
            total += w
            high = w.astype(BF16)
            highs.append(high)
            lows.append((w - high.astype(F32)).astype(BF16))
        sf[...] = total
        at = pl.ds(pl.multiple_of(b * HALF, HALF), HALF)
        both = jnp.dot(jnp.concatenate(highs, axis=1), yf[at, 0 : 2 * LATENT], preferred_element_type=F32)
        rest = jnp.dot(jnp.concatenate(lows, axis=1), yf[at, 0:LATENT], preferred_element_type=F32)
        acc[...] += both[:, :LATENT] + both[:, LATENT:] + rest

    left = lax.broadcasted_iota(jnp.int32, (OWN, LANES), 1) < LANES // 2
    for g in range(2):
        at = slice(g * OWN, (g + 1) * OWN)
        part[g, 0] = acc[at, :]
        part[g, 1] = jnp.where(left, mf[at, :], jnp.sum(sf[at, :], axis=1, keepdims=True))

    def sib_copy():
        return remote(part.at[1 - core], sib, sib_sem.at[0], sib_sem.at[1], (mate, t))

    sib_copy().start()
    mine, mine_stat = part[core, 0], part[core, 1]
    sib_copy().wait_recv()
    m0, s0 = mine_stat[:, 0:1], mine_stat[:, LANES // 2 : LANES // 2 + 1]
    m1, s1 = sib[1, :, 0:1], sib[1, :, LANES // 2 : LANES // 2 + 1]
    best = jnp.maximum(m0, m1)
    e0, e1 = jnp.exp2(m0 - best), jnp.exp2(m1 - best)
    out_ref[own_rows, :] = (e0 * mine + e1 * sib[0]) / (e0 * s0 + e1 * s1)

    def o_view(chunk, block):
        rows = OWN // 2
        return out_ref.at[pl.ds(pl.multiple_of(block * OWN + chunk * rows, rows), rows), :]

    for step in range(NTGT // 2 + 1):
        ring_step(o_view, or_send, or_recv, step)

    ring_drain(t_view, tr_send, tr_recv)
    ring_drain(o_view, or_send, or_recv)
    for chunk in range(2):
        for k in range(1, 4):
            plane_copy(chunk, k, tg.at[slots[chunk]]).wait_send()
    xs_copy().wait_send()
    sib_copy().wait_send()
    for it in range(ITERS):

        @pl.loop(1, NTGT)
        def _(k):
            row_copy(it, k).wait_send()
            pot_copy(it, k).wait_send()

        @pl.loop(1, NSRC)
        def _(k):
            col_copy(it, k).wait_send()

    @pl.loop(1, NTGT)
    def _(k):
        last_copy(k).wait_send()


def on_device(sources, targets, log_source, log_target):
    vmem = pl.BlockSpec(memory_space=pltpu.VMEM)
    dma = pltpu.SemaphoreType.DMA
    sp, tp, bary = pl.pallas_call(
        kernel,
        out_shape=(
            jax.ShapeDtypeStruct((RCH, 1, LANES), F32),
            jax.ShapeDtypeStruct((CCH, LANES), F32),
            jax.ShapeDtypeStruct((ROWS, LATENT), F32),
        ),
        in_specs=[vmem] * 4,
        out_specs=(vmem,) * 3,
        scratch_shapes=[
            pltpu.VMEM((ROWS, 3 * LATENT), BF16),
            pltpu.VMEM((COLS, 3 * LATENT), BF16),
            pltpu.VMEM((COLS, ROWS), F32),
            pltpu.VMEM((ROWS, COLS), F32),
            pltpu.VMEM((COLS, LANES), F32),
            pltpu.VMEM((ROWS, LANES), F32),
            pltpu.VMEM((RCH, 1, LANES), F32),
            pltpu.VMEM((CCH, LANES), F32),
            pltpu.VMEM((ITERS, RCH, 1, LANES), F32),
            pltpu.VMEM((ITERS, NTGT, 1, LANES), F32),
            pltpu.VMEM((ITERS, RCH, 1, LANES), F32),
            pltpu.VMEM((ITERS, CCH, LANES), F32),
            pltpu.VMEM((ITERS, NSRC, CCH, LANES), F32),
            pltpu.VMEM((2, CCH // 2, LANES), F32),
            pltpu.VMEM((NTGT, CCH // 2, LANES), F32),
            pltpu.VMEM((8, NTGT, PIECE, LATENT), F32),
            pltpu.VMEM((2, OWN, LATENT), F32),
            pltpu.VMEM((NTGT * HALF, 3 * LATENT), BF16),
            pltpu.VMEM((2 * OWN, NTGT * HALF), F32),
            pltpu.VMEM((2 * OWN, LANES), F32),
            pltpu.VMEM((2 * OWN, LANES), F32),
            pltpu.VMEM((2 * OWN, LATENT), F32),
            pltpu.VMEM((2, 2, OWN, LATENT), F32),
            pltpu.VMEM((2, OWN, LATENT), F32),
            dma((ITERS, NTGT)), dma((ITERS, NTGT)),
            dma((ITERS, NTGT)), dma((ITERS, NTGT)),
            dma((ITERS, NSRC)), dma((ITERS, NSRC)),
            dma((NTGT,)), dma((NTGT,)),
            dma((2, 2, 8)), dma((2, 2, 8)),
            dma((2, 3)), dma((8,)),
            dma((2, 2, 8)), dma((2, 2, 8)),
            dma((2,)),
            dma((2,)),
        ],
        compiler_params=pltpu.CompilerParams(
            collective_id=0, has_side_effects=True, vmem_limit_bytes=56 * 2**20
        ),
        cost_estimate=pl.CostEstimate(flops=6 * 10**9, bytes_accessed=4 * 2**20, transcendentals=10**7),
        name="coupling",
    )(
        sources,
        targets,
        log_source.reshape(RCH, 1, LANES),
        log_target.reshape(CCH, LANES),
    )
    return sp.reshape(ROWS), tp.reshape(COLS), bary


def solution(mesh):
    in_specs = (P("src", None), P("tgt", None), P("src"), P("tgt"))
    out_specs = (P("src"), P("tgt"), P("src", None))
    return jax.shard_map(
        on_device, mesh=mesh, in_specs=in_specs, out_specs=out_specs, check_vma=False
    )
```

time: 614 us -> 133 us (0.22)
  blocking collectives: 412 us -> 0 us
  Pallas kernels: 0 us -> 126 us
  waiting for transfers between devices: 116 us -> 0 us
  other arithmetic: 43.6 us -> 0 us
  matrix products: 27.9 us -> 0 us
  between operations: 14.2 us -> 0.65 us
    pmax x5 -> x0, blocking collectives: 212 us -> none  [the longest x2 116 us: column_lse(): top_score = lax.pmax(jnp.max(scores, axis=0), 'src')]
    psum x5 -> x0, blocking collectives: 200 us -> none  [the longest x2 117 us: column_lse(): lax.psum(jnp.sum(jnp.exp(scores - top_score[None, :]), axis=0), 'src')]
    pallas_call x0 -> x1, Pallas kernels: none -> 126 us  [on_device(): pl.pallas_call(kernel, out_shape=(jax.ShapeDtypeStruct((RCH, 1, LANES), F...]
    psum x1 -> x0, waiting for transfers between devices: 116 us -> none  [on_device(): total_sum, total_weighted = lax.psum((weight_sum, weighted), 'tgt')]
    dot_general x2 -> x0, matrix products: 27.9 us -> none  [the longest x1 16.9 us: on_device(): jnp.dot(weights, targets, precision=lax.Precision.HIGHEST, preferred_elem...]
    reduce_sum x7 -> x0, other arithmetic: 25 us -> none  [the longest x2 9.09 us: row_lse(): jnp.sum(jnp.exp(scores - top_score[:, None]), axis=1)]
    reduce_max x4 -> x0, other arithmetic: 16 us -> none  [the longest x2 8.01 us: column_lse(): top_score = lax.pmax(jnp.max(scores, axis=0), 'src')]
  transfers between devices with their start and end apart: 1 -> 0, of which waited for: 1 -> 0; matrix products, arithmetic and copies ran while one was open for 1% -> 0% of each run, Pallas kernels for 0% -> 0%
where the time goes in v1:
time: 133 us; the launch traced here: 131 us
  Pallas kernels  126 us (95%)
  local copies, waits for them, and re-layouts  4.22 us (3%)
    pallas_call x1, Pallas kernels, on_device(): pl.pallas_call(kernel, out_shape=(jax.ShapeDtypeStruct((RCH, 1, LANES), F...  126 us
    unnamed x7, local copies, waits for them, and re-layouts  4.22 us

profile of v1, /device:TPU:6, one launch (start us, length us, event | category | flops | bytes accessed | tf_op | source)
XLA Modules:
  0.0 131.1 jit_solution(7355333874393710999)
XLA Ops:
  0.6 126.2 %coupling.1 = (f32[16,1,128]{2,1,0:T(1,128)}, f32[8,128]{1,0:T(8,128)}, f32[2048,128]{1,0:T(8,128)}) custom-call(f32[2048,128]{1,0:T(8,128)} %x_ref.1, f32[1024,128]{1,0:T(8,128)} %y_ref.1, f32[16,1,128]{2,1,0:T(1,128)} %bitcast.6, f32[8,128]{1,0:T(8,128)} %bitcast.7), custom_call_target="tpu_custom_call" | custom-call | flops 6000000000 | bytes 4194304 | tf_op jit(solution)/shard_map/coupling/pallas_call | solution.py:413
  126.8 0.0 copy-start
  126.9 0.7 copy-done
  127.5 0.0 copy-start.1
  127.6 0.6 copy.10
  128.2 0.1 copy-done.1
  128.2 0.6 copy.11
  128.8 2.3 %copy.12 = f32[2048,128]{1,0:T(8,128)} copy(f32[2048,128]{1,0:T(8,128)} %get-tuple-element.14) | data formatting | bytes 2097152
Async XLA Ops:
  126.8 0.7 copy-start
  127.5 0.7 copy-start.1

commit v2 on v1

v2 whole, which is shorter than its diff:
```python
import math

import jax
import jax.numpy as jnp
from jax import lax
from jax.experimental import pallas as pl
from jax.experimental.pallas import tpu as pltpu
from jax.sharding import PartitionSpec as P

ITERS = 2
LATENT = 128
LANES = 128
LOG2E = math.log2(math.e)
LN2 = math.log(2.0)
MESH = pl.DeviceIdType.MESH

NSRC, NTGT = 32, 16
GRID_X, GRID_Y = 4, 4
ROWS, COLS = 2048, 1024
RCH, CCH = ROWS // LANES, COLS // LANES
OWN = ROWS // NTGT
MATES = GRID_X * 2
PIECE = COLS // MATES
F32, BF16 = jnp.float32, jnp.bfloat16


def split3(v, order):
    high = v.astype(BF16)
    low = (v - high.astype(F32)).astype(BF16)
    return jnp.concatenate([(high, low)[k] for k in order], axis=1)


def nt_dot(a, b):
    return lax.dot_general(a, b, (((1,), (1,)), ((), ())), preferred_element_type=F32)


def spread(row):
    return jnp.broadcast_to(row, (LANES, LANES)).T


def lse_pass(z_ref, b_ref, rows, cols, put):
    width, depth = 4, 64

    def load(block, col, k):
        at = pl.ds(pl.multiple_of(block * depth, depth), depth)
        lane = pl.multiple_of(col * width * LANES + k * LANES, LANES)
        return (z_ref[at, pl.ds(lane, LANES)] + b_ref[at, :]).reshape(depth // 8, 8, LANES)

    @pl.loop(0, cols // (width * LANES))
    def _(col):
        def top(block, acc):
            return tuple(jnp.maximum(acc[k], jnp.max(load(block, col, k), axis=0)) for k in range(width))

        start = tuple(jnp.full((8, LANES), -jnp.inf, F32) for _ in range(width))
        tops = lax.fori_loop(0, rows // depth, top, start)
        tops = [jnp.max(v, axis=0, keepdims=True) for v in tops]

        def total(block, acc):
            return tuple(
                acc[k] + jnp.sum(jnp.exp2(load(block, col, k) - tops[k].reshape(1, 1, LANES)), axis=0)
                for k in range(width)
            )

        sums = lax.fori_loop(0, rows // depth, total, tuple(jnp.zeros((8, LANES), F32) for _ in range(width)))
        for k in range(width):
            put(col * width + k, tops[k] + LOG2E * jnp.log(jnp.sum(sums[k], axis=0, keepdims=True)))


def combine(parts):
    top = jnp.max(parts, axis=0)
    return top + LOG2E * jnp.log(jnp.sum(jnp.exp2(parts - top[None]), axis=0))


def kernel(
    x_ref, y_ref, la_ref, lb_ref, sp_ref, tp_ref, out_ref,
    xa, ya, zt, z, qb, pb, nx, ny,
    l_row, rs, pg, l_col, cr, qs, qg, tg, xs, xf, yf, mf, sf, acc, part, shares,
    rs_sem, pg_sem, cr_sem, qg_sem, tr_send, tr_recv, or_send, or_recv, xs_sem, part_sem,
):
    s, t = lax.axis_index("src"), lax.axis_index("tgt")
    gx, gy, core = s // (GRID_Y * 2), lax.rem(s // 2, GRID_Y), lax.rem(s, 2)
    me = gx * 2 + core

    def z_peer(k):
        return lax.rem(t + k, NTGT)

    def s_peer(k):
        return lax.rem(s + k, NSRC)

    def mate(e):
        return ((e // 2) * GRID_Y + gy) * 2 + lax.rem(e, 2)

    barrier = pltpu.get_barrier_semaphore()

    @pl.loop(1, NTGT)
    def _(k):
        pl.semaphore_signal(barrier, inc=1, device_id=(s, z_peer(k)), device_id_type=MESH)

    @pl.loop(1, NSRC)
    def _(k):
        pl.semaphore_signal(barrier, inc=1, device_id=(s_peer(k), t), device_id_type=MESH)

    def remote(src, dst, send, recv, device):
        return pltpu.make_async_remote_copy(
            src_ref=src, dst_ref=dst, send_sem=send, recv_sem=recv, device_id=device, device_id_type=MESH
        )

    def wait_bytes(ref, sem):
        remote(ref, ref, sem, sem, (s, t)).wait_recv()

    @pl.loop(0, ROWS // 256)
    def _(k):
        at = pl.ds(pl.multiple_of(k * 256, 256), 256)
        xa[at, :] = split3(x_ref[at, :] * (2.0 * LOG2E), (0, 0, 1))

    @pl.loop(0, COLS // 256)
    def _(k):
        at = pl.ds(pl.multiple_of(k * 256, 256), 256)
        y = y_ref[at, :]
        ya[at, :] = split3(y, (0, 1, 0))
        qb[at, :] = jnp.broadcast_to(-LOG2E * jnp.sum(y * y, axis=1, keepdims=True), (256, LANES))

    tg[t] = y_ref[pl.ds(pl.multiple_of(me * PIECE, PIECE), PIECE), :]
    own_rows = pl.ds(pl.multiple_of(t * OWN, OWN), OWN)
    xs[me] = x_ref[own_rows, :]

    pl.semaphore_wait(barrier, NTGT - 1 + NSRC - 1)

    def hops(way, chunk):
        return NTGT // 2 - (way ^ chunk)

    def ring_step(view, send, recv, step):
        for chunk in range(2):
            for way in range(2):
                if step > hops(way, chunk):
                    continue
                block = lax.rem(t + (NTGT - step if way == 0 else step), NTGT)
                ref = view(chunk, block)
                if step > 0:
                    wait_bytes(ref, recv.at[way, chunk, step - 1])
                if step < hops(way, chunk):
                    to = lax.rem(t + (1 if way == 0 else NTGT - 1), NTGT)
                    remote(ref, ref, send.at[way, chunk], recv.at[way, chunk, step], (s, to)).start()

    def t_view(chunk, block):
        return tg.at[block, pl.ds(chunk * (PIECE // 2), PIECE // 2), :]

    def t_step(step):
        ring_step(t_view, tr_send, tr_recv, step)

    t_step(0)

    @pl.loop(1, MATES)
    def _(k):
        to = mate(lax.rem(me + k, MATES))
        remote(xs.at[me], xs.at[me], xs_sem.at[0], xs_sem.at[1], (to, t)).start()

    @pl.loop(0, ROWS // 256)
    def _(k):
        at = pl.ds(pl.multiple_of(k * 256, 256), 256)
        zt[:, at] = nt_dot(ya[...], xa[at, :])

    t_step(1)

    for it in range(ITERS):

        def put_row(chunk, value):
            l_row[it, chunk] = value

        lse_pass(zt, qb, COLS, ROWS, put_row)
        rs[it, t] = l_row[it, t]

        @pl.loop(1, NTGT)
        def _(k):
            to = z_peer(k)
            remote(l_row.at[it, to], rs.at[it, t], rs_sem.at[it, 0], rs_sem.at[it, 1], (s, to)).start()

        if it == 0:
            t_step(2)
            for half in range(2):
                @pl.loop(half * 2, half * 2 + 2)
                def _(k):
                    at = pl.ds(pl.multiple_of(k * 256, 256), 256)
                    z[:, at] = nt_dot(xa[...], ya[at, :])

                if half == 0:
                    t_step(3)
        else:
            t_step(7)

        wait_bytes(rs.at[it, pl.ds(0, NTGT - 1)], rs_sem.at[it, 1])
        pg[it, t] = LOG2E * la_ref[t] - combine(rs[it])

        @pl.loop(1, NTGT)
        def _(k):
            remote(pg.at[it, t], pg.at[it, t], pg_sem.at[it, 0], pg_sem.at[it, 1], (s, z_peer(k))).start()

        if it == 0:
            t_step(4)

            for k in range(RCH):
                block = x_ref[k * LANES : (k + 1) * LANES, :]
                nx[k] = jnp.sum((block * block).T, axis=0, keepdims=True)
            for k in range(CCH):
                ny[k : k + 1, :] = qb[k * LANES : (k + 1) * LANES, :].T[0:1, :] * (-LN2)
        else:
            t_step(8)

        wait_bytes(pg.at[it, pl.ds(0, NTGT - 1)], pg_sem.at[it, 1])
        for k in range(RCH):
            pb[k * LANES : (k + 1) * LANES, :] = spread(pg[it, k])

        def put_col(chunk, value):
            l_col[it, pl.ds(chunk, 1), :] = value

        lse_pass(z, pb, ROWS, COLS, put_col)

        @pl.loop(1, NSRC)
        def _(k):
            remote(l_col.at[it], cr.at[it, s], cr_sem.at[it, 0], cr_sem.at[it, 1], (s_peer(k), t)).start()

        cr[it, s] = l_col[it]
        if it == 0:
            t_step(5)
        else:
            sp_ref[...] = pg[it] * LN2 + nx[...]
            wait_bytes(xs.at[pl.ds(0, MATES - 1)], xs_sem.at[1])

            @pl.loop(0, MATES)
            def _(e):
                at = pl.ds(pl.multiple_of(e * OWN, OWN), OWN)
                xf[at, :] = split3(xs[e] * (2.0 * LOG2E), (0, 0, 1))

            @pl.loop(0, NTGT // 2)
            def _(b):
                at = pl.ds(pl.multiple_of(b * 2 * PIECE, 2 * PIECE), 2 * PIECE)
                yf[at, :] = split3(tg[pl.ds(b * 2, 2)].reshape(2 * PIECE, LATENT), (0, 1, 0))
                zt[:, at] = nt_dot(xf[...], yf[at, :])

        wait_bytes(cr.at[it, pl.ds(0, NSRC - 1)], cr_sem.at[it, 1])
        q = LOG2E * lb_ref[...] - combine(cr[it])
        if it == 0:
            for k in range(CCH):
                qb[k * LANES : (k + 1) * LANES, :] = spread(q[k : k + 1, :])
            t_step(6)

    for k in range(CCH):
        qs[k] = q[k : k + 1, :]
    qg[t] = qs[me]

    @pl.loop(1, NTGT)
    def _(k):
        remote(qs.at[me], qg.at[t], qg_sem.at[0], qg_sem.at[1], (s, z_peer(k))).start()

    tp_ref[...] = q * LN2 + ny[...]
    wait_bytes(qg.at[pl.ds(0, NTGT - 1)], qg_sem.at[1])

    depth = 64
    for far in (2, 1, 3, 0):
        chip = lax.rem(gx + far, GRID_X)
        base = chip * 2 * OWN

        @pl.loop(0, 2 * OWN // depth)
        def _(r):
            at = pl.ds(pl.multiple_of(base + r * depth, depth), depth)
            best = zt[at, 0:LANES] + qg[0]
            for b in range(1, NTGT):
                best = jnp.maximum(best, zt[at, b * LANES : (b + 1) * LANES] + qg[b])
            to = pl.ds(pl.multiple_of(r * depth, depth), depth)
            mf[to, :] = jnp.broadcast_to(jnp.max(best, axis=1, keepdims=True), (depth, LANES))

        sf[...] = jnp.zeros_like(sf)
        acc[...] = jnp.zeros_like(acc)
        at = pl.ds(pl.multiple_of(base, 2 * OWN), 2 * OWN)
        group = 4

        @pl.loop(0, NTGT // group)
        def _(b):
            highs, lows = [], []
            total = sf[...]
            for k in range(group):
                lane = pl.ds(pl.multiple_of((b * group + k) * LANES, LANES), LANES)
                w = jnp.exp2(zt[at, lane] + qg[b * group + k] - mf[...])
                total += w
                high = w.astype(BF16)
                highs.append(high)
                lows.append((w - high.astype(F32)).astype(BF16))
            sf[...] = total
            ys = pl.ds(pl.multiple_of(b * group * LANES, group * LANES), group * LANES)
            both = jnp.dot(jnp.concatenate(highs, axis=1), yf[ys, 0 : 2 * LATENT], preferred_element_type=F32)
            rest = jnp.dot(jnp.concatenate(lows, axis=1), yf[ys, 0:LATENT], preferred_element_type=F32)
            acc[...] += both[:, :LATENT] + both[:, LATENT:] + rest

        for g in range(2):
            rows = slice(g * OWN, (g + 1) * OWN)
            to = chip * 2 + g
            part[to, 0:OWN, :] = acc[rows, :]
            part[to, OWN : OWN + 1, :] = mf[rows, :].T[0:1, :]
            part[to, OWN + 1 : OWN + 2, :] = jnp.sum(sf[rows, :].T, axis=0, keepdims=True)

            def send():
                remote(part.at[to], shares.at[me], part_sem.at[0], part_sem.at[1], (mate(to), t)).start()

            if far == 0:
                pl.when(core != g)(send)
            else:
                send()

    shares[me, 0 : OWN + 2, :] = part[me, 0 : OWN + 2, :]
    wait_bytes(shares.at[pl.ds(0, MATES - 1)], part_sem.at[1])
    tops = [shares[e, OWN : OWN + 1, :] for e in range(MATES)]
    best = tops[0]
    for v in tops[1:]:
        best = jnp.maximum(best, v)
    scales = [jnp.exp2(v - best) for v in tops]
    total = sum(scales[e] * shares[e, OWN + 1 : OWN + 2, :] for e in range(MATES))
    out = jnp.zeros((OWN, LATENT), F32)
    for e in range(MATES):
        out += spread(scales[e] / total) * shares[e, 0:OWN, :]
    out_ref[own_rows, :] = out

    def o_view(chunk, block):
        rows = OWN // 2
        return out_ref.at[pl.ds(pl.multiple_of(block * OWN + chunk * rows, rows), rows), :]

    for step in range(NTGT // 2 + 1):
        ring_step(o_view, or_send, or_recv, step)

    for chunk in range(2):
        for way in range(2):
            n = hops(way, chunk)
            wait_bytes(tg.at[pl.ds(0, n), pl.ds(0, PIECE // 2), :], tr_send.at[way, chunk])
            wait_bytes(out_ref.at[pl.ds(0, n * (OWN // 2)), :], or_send.at[way, chunk])
    wait_bytes(xs.at[pl.ds(0, MATES - 1)], xs_sem.at[0])
    wait_bytes(part.at[pl.ds(0, MATES - 1)], part_sem.at[0])
    for it in range(ITERS):
        wait_bytes(rs.at[it, pl.ds(0, NTGT - 1)], rs_sem.at[it, 0])
        wait_bytes(pg.at[it, pl.ds(0, NTGT - 1)], pg_sem.at[it, 0])
        wait_bytes(cr.at[it, pl.ds(0, NSRC - 1)], cr_sem.at[it, 0])
    wait_bytes(qg.at[pl.ds(0, NTGT - 1)], qg_sem.at[0])


def on_device(sources, targets, log_source, log_target):
    vmem = pl.BlockSpec(memory_space=pltpu.VMEM)
    dma = pltpu.SemaphoreType.DMA
    sp, tp, bary = pl.pallas_call(
        kernel,
        out_shape=(
            jax.ShapeDtypeStruct((RCH, 1, LANES), F32),
            jax.ShapeDtypeStruct((CCH, LANES), F32),
            jax.ShapeDtypeStruct((ROWS, LATENT), F32),
        ),
        in_specs=[vmem] * 4,
        out_specs=(vmem,) * 3,
        scratch_shapes=[
            pltpu.VMEM((ROWS, 3 * LATENT), BF16),
            pltpu.VMEM((COLS, 3 * LATENT), BF16),
            pltpu.VMEM((COLS, ROWS), F32),
            pltpu.VMEM((ROWS, COLS), F32),
            pltpu.VMEM((COLS, LANES), F32),
            pltpu.VMEM((ROWS, LANES), F32),
            pltpu.VMEM((RCH, 1, LANES), F32),
            pltpu.VMEM((CCH, LANES), F32),
            pltpu.VMEM((ITERS, RCH, 1, LANES), F32),
            pltpu.VMEM((ITERS, NTGT, 1, LANES), F32),
            pltpu.VMEM((ITERS, RCH, 1, LANES), F32),
            pltpu.VMEM((ITERS, CCH, LANES), F32),
            pltpu.VMEM((ITERS, NSRC, CCH, LANES), F32),
            pltpu.VMEM((CCH, 1, LANES), F32),
            pltpu.VMEM((NTGT, 1, LANES), F32),
            pltpu.VMEM((NTGT, PIECE, LATENT), F32),
            pltpu.VMEM((MATES, OWN, LATENT), F32),
            pltpu.VMEM((MATES * OWN, 3 * LATENT), BF16),
            pltpu.VMEM((NTGT * PIECE, 3 * LATENT), BF16),
            pltpu.VMEM((2 * OWN, LANES), F32),
            pltpu.VMEM((2 * OWN, LANES), F32),
            pltpu.VMEM((2 * OWN, LATENT), F32),
            pltpu.VMEM((MATES, OWN + 8, LATENT), F32),
            pltpu.VMEM((MATES, OWN + 8, LATENT), F32),
            dma((ITERS, 2)),
            dma((ITERS, 2)),
            dma((ITERS, 2)),
            dma((2,)),
            dma((2, 2)), dma((2, 2, 8)),
            dma((2, 2)), dma((2, 2, 8)),
            dma((2,)),
            dma((2,)),
        ],
        compiler_params=pltpu.CompilerParams(
            collective_id=0, has_side_effects=True, vmem_limit_bytes=56 * 2**20
        ),
        cost_estimate=pl.CostEstimate(flops=6 * 10**9, bytes_accessed=4 * 2**20, transcendentals=10**7),
        name="coupling",
    )(
        sources,
        targets,
        log_source.reshape(RCH, 1, LANES),
        log_target.reshape(CCH, LANES),
    )
    return sp.reshape(ROWS), tp.reshape(COLS), bary


def solution(mesh):
    in_specs = (P("src", None), P("tgt", None), P("src"), P("tgt"))
    out_specs = (P("src"), P("tgt"), P("src", None))
    return jax.shard_map(
        on_device, mesh=mesh, in_specs=in_specs, out_specs=out_specs, check_vma=False
    )
```

time: 133 us -> 126 us (0.947)
  Pallas kernels: 126 us -> 120 us
    pallas_call x1, Pallas kernels: 126 us -> 120 us  [on_device(): pl.pallas_call(kernel, out_shape=(jax.ShapeDtypeStruct((RCH, 1, LANES), F...]
where the time goes in v2:
time: 126 us; the launch traced here: 125 us
  Pallas kernels  120 us (95%)
  local copies, waits for them, and re-layouts  4.22 us (3%)
    pallas_call x1, Pallas kernels, on_device(): pl.pallas_call(kernel, out_shape=(jax.ShapeDtypeStruct((RCH, 1, LANES), F...  120 us
    unnamed x7, local copies, waits for them, and re-layouts  4.22 us

profile of v2, /device:TPU:6, one launch (start us, length us, event | category | flops | bytes accessed | tf_op | source)
XLA Modules:
  0.0 125.3 jit_solution(8130822396185431600)
XLA Ops:
  0.6 120.4 %coupling.1 = (f32[16,1,128]{2,1,0:T(1,128)}, f32[8,128]{1,0:T(8,128)}, f32[2048,128]{1,0:T(8,128)}) custom-call(f32[2048,128]{1,0:T(8,128)} %x_ref.1, f32[1024,128]{1,0:T(8,128)} %y_ref.1, f32[16,1,128]{2,1,0:T(1,128)} %bitcast.6, f32[8,128]{1,0:T(8,128)} %bitcast.7), custom_call_target="tpu_custom_call" | custom-call | flops 6000000000 | bytes 4194304 | tf_op jit(solution)/shard_map/coupling/pallas_call | solution.py:346
  121.1 0.0 copy-start
  121.1 0.7 copy-done
  121.8 0.0 copy-start.1
  121.8 0.6 copy.10
  122.4 0.1 copy-done.1
  122.4 0.6 copy.11
  123.0 2.3 %copy.12 = f32[2048,128]{1,0:T(8,128)} copy(f32[2048,128]{1,0:T(8,128)} %get-tuple-element.14) | data formatting | bytes 2097152
Async XLA Ops:
  121.1 0.7 copy-start
  121.8 0.7 copy-start.1

commit v3 on v2

--- a/solution.py
+++ b/solution.py
@@ -24,14 +24,14 @@
 F32, BF16 = jnp.float32, jnp.bfloat16
 
 
-def split3(v, order):
+def split3(v, order, axis=1):
     high = v.astype(BF16)
     low = (v - high.astype(F32)).astype(BF16)
-    return jnp.concatenate([(high, low)[k] for k in order], axis=1)
-
-
-def nt_dot(a, b):
-    return lax.dot_general(a, b, (((1,), (1,)), ((), ())), preferred_element_type=F32)
+    return jnp.concatenate([(high, low)[k] for k in order], axis=axis)
+
+
+def dot(a, b):
+    return jnp.dot(a, b, preferred_element_type=F32)
 
 
 def spread(row):
@@ -39,31 +39,29 @@
 
 
 def lse_pass(z_ref, b_ref, rows, cols, put):
-    width, depth = 4, 64
-
-    def load(block, col, k):
-        at = pl.ds(pl.multiple_of(block * depth, depth), depth)
-        lane = pl.multiple_of(col * width * LANES + k * LANES, LANES)
-        return (z_ref[at, pl.ds(lane, LANES)] + b_ref[at, :]).reshape(depth // 8, 8, LANES)
+    width, depth = 2, 128
 
     @pl.loop(0, cols // (width * LANES))
     def _(col):
-        def top(block, acc):
-            return tuple(jnp.maximum(acc[k], jnp.max(load(block, col, k), axis=0)) for k in range(width))
-
-        start = tuple(jnp.full((8, LANES), -jnp.inf, F32) for _ in range(width))
-        tops = lax.fori_loop(0, rows // depth, top, start)
-        tops = [jnp.max(v, axis=0, keepdims=True) for v in tops]
-
-        def total(block, acc):
-            return tuple(
-                acc[k] + jnp.sum(jnp.exp2(load(block, col, k) - tops[k].reshape(1, 1, LANES)), axis=0)
-                for k in range(width)
-            )
-
-        sums = lax.fori_loop(0, rows // depth, total, tuple(jnp.zeros((8, LANES), F32) for _ in range(width)))
+        def block(n, state):
+            at = pl.ds(pl.multiple_of(n * depth, depth), depth)
+            out = []
+            for k in range(width):
+                top, total = state[k]
+                lane = pl.multiple_of(col * width * LANES + k * LANES, LANES)
+                v = (z_ref[at, pl.ds(lane, LANES)] + b_ref[at, :]).reshape(depth // 8, 8, LANES)
+                new = jnp.maximum(top, jnp.max(v, axis=0))
+                total = total * jnp.exp2(top - new) + jnp.sum(jnp.exp2(v - new[None]), axis=0)
+                out.append((new, total))
+            return tuple(out)
+
+        start = (jnp.full((8, LANES), -jnp.inf, F32), jnp.zeros((8, LANES), F32))
+        state = lax.fori_loop(0, rows // depth, block, (start,) * width, unroll=4)
         for k in range(width):
-            put(col * width + k, tops[k] + LOG2E * jnp.log(jnp.sum(sums[k], axis=0, keepdims=True)))
+            top, total = state[k]
+            best = jnp.max(top, axis=0, keepdims=True)
+            total = jnp.sum(total * jnp.exp2(top - best), axis=0, keepdims=True)
+            put(col * width + k, best + LOG2E * jnp.log(total))
 
 
 def combine(parts):
@@ -73,7 +71,7 @@
 
 def kernel(
     x_ref, y_ref, la_ref, lb_ref, sp_ref, tp_ref, out_ref,
-    xa, ya, zt, z, qb, pb, nx, ny,
+    xa, xt, ya, yt, zt, z, qb, pb, nx, ny,
     l_row, rs, pg, l_col, cr, qs, qg, tg, xs, xf, yf, mf, sf, acc, part, shares,
     rs_sem, pg_sem, cr_sem, qg_sem, tr_send, tr_recv, or_send, or_recv, xs_sem, part_sem,
 ):
@@ -108,21 +106,32 @@
     def wait_bytes(ref, sem):
         remote(ref, ref, sem, sem, (s, t)).wait_recv()
 
-    @pl.loop(0, ROWS // 256)
-    def _(k):
-        at = pl.ds(pl.multiple_of(k * 256, 256), 256)
-        xa[at, :] = split3(x_ref[at, :] * (2.0 * LOG2E), (0, 0, 1))
-
-    @pl.loop(0, COLS // 256)
-    def _(k):
-        at = pl.ds(pl.multiple_of(k * 256, 256), 256)
+    @pl.loop(0, RCH, unroll=2)
+    def _(k):
+        at = pl.ds(pl.multiple_of(k * LANES, LANES), LANES)
+        x = x_ref[at, :]
+        turned = x.T
+        nx[k] = jnp.sum(turned * turned, axis=0, keepdims=True)
+        xa[at, :] = split3(x * (2.0 * LOG2E), (0, 0, 1))
+        xt[:, at] = split3(turned * (2.0 * LOG2E), (0, 0, 1), axis=0)
+
+    for k in range(CCH):
+        at = slice(k * LANES, (k + 1) * LANES)
         y = y_ref[at, :]
+        turned = y.T
+        ny[k : k + 1, :] = jnp.sum(turned * turned, axis=0, keepdims=True)
         ya[at, :] = split3(y, (0, 1, 0))
-        qb[at, :] = jnp.broadcast_to(-LOG2E * jnp.sum(y * y, axis=1, keepdims=True), (256, LANES))
+        yt[:, at] = split3(turned, (0, 1, 0), axis=0)
+        qb[at, :] = spread(-LOG2E * ny[k : k + 1, :])
 
     tg[t] = y_ref[pl.ds(pl.multiple_of(me * PIECE, PIECE), PIECE), :]
     own_rows = pl.ds(pl.multiple_of(t * OWN, OWN), OWN)
     xs[me] = x_ref[own_rows, :]
+
+    @pl.loop(0, ROWS // 256)
+    def _(k):
+        at = pl.ds(pl.multiple_of(k * 256, 256), 256)
+        zt[:, at] = dot(ya[...], xt[:, at])
 
     pl.semaphore_wait(barrier, NTGT - 1 + NSRC - 1)
 
@@ -155,13 +164,6 @@
         to = mate(lax.rem(me + k, MATES))
         remote(xs.at[me], xs.at[me], xs_sem.at[0], xs_sem.at[1], (to, t)).start()
 
-    @pl.loop(0, ROWS // 256)
-    def _(k):
-        at = pl.ds(pl.multiple_of(k * 256, 256), 256)
-        zt[:, at] = nt_dot(ya[...], xa[at, :])
-
-    t_step(1)
-
     for it in range(ITERS):
 
         def put_row(chunk, value):
@@ -176,15 +178,14 @@
             remote(l_row.at[it, to], rs.at[it, t], rs_sem.at[it, 0], rs_sem.at[it, 1], (s, to)).start()
 
         if it == 0:
-            t_step(2)
+            t_step(1)
             for half in range(2):
                 @pl.loop(half * 2, half * 2 + 2)
                 def _(k):
                     at = pl.ds(pl.multiple_of(k * 256, 256), 256)
-                    z[:, at] = nt_dot(xa[...], ya[at, :])
-
-                if half == 0:
-                    t_step(3)
+                    z[:, at] = dot(xa[...], yt[:, at])
+
+                t_step(2 + half)
         else:
             t_step(7)
 
@@ -195,17 +196,7 @@
         def _(k):
             remote(pg.at[it, t], pg.at[it, t], pg_sem.at[it, 0], pg_sem.at[it, 1], (s, z_peer(k))).start()
 
-        if it == 0:
-            t_step(4)
-
-            for k in range(RCH):
-                block = x_ref[k * LANES : (k + 1) * LANES, :]
-                nx[k] = jnp.sum((block * block).T, axis=0, keepdims=True)
-            for k in range(CCH):
-                ny[k : k + 1, :] = qb[k * LANES : (k + 1) * LANES, :].T[0:1, :] * (-LN2)
-        else:
-            t_step(8)
-
+        t_step(4 if it == 0 else 8)
         wait_bytes(pg.at[it, pl.ds(0, NTGT - 1)], pg_sem.at[it, 1])
         for k in range(RCH):
             pb[k * LANES : (k + 1) * LANES, :] = spread(pg[it, k])
@@ -234,8 +225,9 @@
             @pl.loop(0, NTGT // 2)
             def _(b):
                 at = pl.ds(pl.multiple_of(b * 2 * PIECE, 2 * PIECE), 2 * PIECE)
-                yf[at, :] = split3(tg[pl.ds(b * 2, 2)].reshape(2 * PIECE, LATENT), (0, 1, 0))
-                zt[:, at] = nt_dot(xf[...], yf[at, :])
+                y = tg[pl.ds(b * 2, 2)].reshape(2 * PIECE, LATENT)
+                yf[at, :] = split3(y, (0, 1))
+                zt[:, at] = dot(xf[...], split3(y.T, (0, 1, 0), axis=0))
 
         wait_bytes(cr.at[it, pl.ds(0, NSRC - 1)], cr_sem.at[it, 1])
         q = LOG2E * lb_ref[...] - combine(cr[it])
@@ -354,7 +346,9 @@
         out_specs=(vmem,) * 3,
         scratch_shapes=[
             pltpu.VMEM((ROWS, 3 * LATENT), BF16),
+            pltpu.VMEM((3 * LATENT, ROWS), BF16),
             pltpu.VMEM((COLS, 3 * LATENT), BF16),
+            pltpu.VMEM((3 * LATENT, COLS), BF16),
             pltpu.VMEM((COLS, ROWS), F32),
             pltpu.VMEM((ROWS, COLS), F32),
             pltpu.VMEM((COLS, LANES), F32),
@@ -371,7 +365,7 @@
             pltpu.VMEM((NTGT, PIECE, LATENT), F32),
             pltpu.VMEM((MATES, OWN, LATENT), F32),
             pltpu.VMEM((MATES * OWN, 3 * LATENT), BF16),
-            pltpu.VMEM((NTGT * PIECE, 3 * LATENT), BF16),
+            pltpu.VMEM((NTGT * PIECE, 2 * LATENT), BF16),
             pltpu.VMEM((2 * OWN, LANES), F32),
             pltpu.VMEM((2 * OWN, LANES), F32),
             pltpu.VMEM((2 * OWN, LATENT), F32),

time: 126 us -> 117 us (0.929)
  Pallas kernels: 120 us -> 112 us
    pallas_call x1, Pallas kernels: 120 us -> 112 us  [on_device(): pl.pallas_call(kernel, out_shape=(jax.ShapeDtypeStruct((RCH, 1, LANES), F...]
where the time goes in v3:
time: 117 us
  Pallas kernels  112 us (96%)
  local copies, waits for them, and re-layouts  4.22 us (4%)
    pallas_call x1, Pallas kernels, on_device(): pl.pallas_call(kernel, out_shape=(jax.ShapeDtypeStruct((RCH, 1, LANES), F...  112 us
    unnamed x7, local copies, waits for them, and re-layouts  4.22 us

profile of v3, /device:TPU:6, one launch (start us, length us, event | category | flops | bytes accessed | tf_op | source)
XLA Modules:
  0.0 117.0 jit_solution(1334314826072876881)
XLA Ops:
  0.6 112.2 %coupling.1 = (f32[16,1,128]{2,1,0:T(1,128)}, f32[8,128]{1,0:T(8,128)}, f32[2048,128]{1,0:T(8,128)}) custom-call(f32[2048,128]{1,0:T(8,128)} %x_ref.1, f32[1024,128]{1,0:T(8,128)} %y_ref.1, f32[16,1,128]{2,1,0:T(1,128)} %bitcast.6, f32[8,128]{1,0:T(8,128)} %bitcast.7), custom_call_target="tpu_custom_call" | custom-call | flops 6000000000 | bytes 4194304 | tf_op jit(solution)/shard_map/coupling/pallas_call | solution.py:338
  112.8 0.0 copy-start
  112.8 0.7 copy-done
  113.5 0.0 copy-start.1
  113.5 0.6 copy.10
  114.1 0.1 copy-done.1
  114.2 0.6 copy.11
  114.8 2.3 %copy.12 = f32[2048,128]{1,0:T(8,128)} copy(f32[2048,128]{1,0:T(8,128)} %get-tuple-element.14) | data formatting | bytes 2097152
Async XLA Ops:
  112.8 0.7 copy-start
  113.5 0.7 copy-start.1

commit v4 on v3

--- a/solution.py
+++ b/solution.py
@@ -72,8 +72,8 @@
 def kernel(
     x_ref, y_ref, la_ref, lb_ref, sp_ref, tp_ref, out_ref,
     xa, xt, ya, yt, zt, z, qb, pb, nx, ny,
-    l_row, rs, pg, l_col, cr, qs, qg, tg, xs, xf, yf, mf, sf, acc, part, shares,
-    rs_sem, pg_sem, cr_sem, qg_sem, tr_send, tr_recv, or_send, or_recv, xs_sem, part_sem,
+    l_row, rs, l_col, cr, qs, qg, tg, xs, xf, yf, mf, sf, acc, part, shares,
+    rs_sem, cr_sem, qg_sem, tr_send, tr_recv, or_send, or_recv, xs_sem, part_sem,
 ):
     s, t = lax.axis_index("src"), lax.axis_index("tgt")
     gx, gy, core = s // (GRID_Y * 2), lax.rem(s // 2, GRID_Y), lax.rem(s, 2)
@@ -111,7 +111,7 @@
         at = pl.ds(pl.multiple_of(k * LANES, LANES), LANES)
         x = x_ref[at, :]
         turned = x.T
-        nx[k] = jnp.sum(turned * turned, axis=0, keepdims=True)
+        nx[pl.ds(k, 1), :] = jnp.sum(turned * turned, axis=0, keepdims=True)
         xa[at, :] = split3(x * (2.0 * LOG2E), (0, 0, 1))
         xt[:, at] = split3(turned * (2.0 * LOG2E), (0, 0, 1), axis=0)
 
@@ -167,16 +167,15 @@
     for it in range(ITERS):
 
         def put_row(chunk, value):
-            l_row[it, chunk] = value
+            l_row[it, pl.ds(chunk, 1), :] = value
 
         lse_pass(zt, qb, COLS, ROWS, put_row)
-        rs[it, t] = l_row[it, t]
 
         @pl.loop(1, NTGT)
         def _(k):
-            to = z_peer(k)
-            remote(l_row.at[it, to], rs.at[it, t], rs_sem.at[it, 0], rs_sem.at[it, 1], (s, to)).start()
-
+            remote(l_row.at[it], rs.at[it, t], rs_sem.at[it, 0], rs_sem.at[it, 1], (s, z_peer(k))).start()
+
+        rs[it, t] = l_row[it]
         if it == 0:
             t_step(1)
             for half in range(2):
@@ -190,16 +189,10 @@
             t_step(7)
 
         wait_bytes(rs.at[it, pl.ds(0, NTGT - 1)], rs_sem.at[it, 1])
-        pg[it, t] = LOG2E * la_ref[t] - combine(rs[it])
-
-        @pl.loop(1, NTGT)
-        def _(k):
-            remote(pg.at[it, t], pg.at[it, t], pg_sem.at[it, 0], pg_sem.at[it, 1], (s, z_peer(k))).start()
-
+        row_pot = LOG2E * la_ref[...] - combine(rs[it])
+        for k in range(RCH):
+            pb[k * LANES : (k + 1) * LANES, :] = spread(row_pot[k : k + 1, :])
         t_step(4 if it == 0 else 8)
-        wait_bytes(pg.at[it, pl.ds(0, NTGT - 1)], pg_sem.at[it, 1])
-        for k in range(RCH):
-            pb[k * LANES : (k + 1) * LANES, :] = spread(pg[it, k])
 
         def put_col(chunk, value):
             l_col[it, pl.ds(chunk, 1), :] = value
@@ -214,7 +207,7 @@
         if it == 0:
             t_step(5)
         else:
-            sp_ref[...] = pg[it] * LN2 + nx[...]
+            sp_ref[...] = row_pot * LN2 + nx[...]
             wait_bytes(xs.at[pl.ds(0, MATES - 1)], xs_sem.at[1])
 
             @pl.loop(0, MATES)
@@ -327,7 +320,6 @@
     wait_bytes(part.at[pl.ds(0, MATES - 1)], part_sem.at[0])
     for it in range(ITERS):
         wait_bytes(rs.at[it, pl.ds(0, NTGT - 1)], rs_sem.at[it, 0])
-        wait_bytes(pg.at[it, pl.ds(0, NTGT - 1)], pg_sem.at[it, 0])
         wait_bytes(cr.at[it, pl.ds(0, NSRC - 1)], cr_sem.at[it, 0])
     wait_bytes(qg.at[pl.ds(0, NTGT - 1)], qg_sem.at[0])
 
@@ -338,7 +330,7 @@
     sp, tp, bary = pl.pallas_call(
         kernel,
         out_shape=(
-            jax.ShapeDtypeStruct((RCH, 1, LANES), F32),
+            jax.ShapeDtypeStruct((RCH, LANES), F32),
             jax.ShapeDtypeStruct((CCH, LANES), F32),
             jax.ShapeDtypeStruct((ROWS, LATENT), F32),
         ),
@@ -353,11 +345,10 @@
             pltpu.VMEM((ROWS, COLS), F32),
             pltpu.VMEM((COLS, LANES), F32),
             pltpu.VMEM((ROWS, LANES), F32),
-            pltpu.VMEM((RCH, 1, LANES), F32),
+            pltpu.VMEM((RCH, LANES), F32),
             pltpu.VMEM((CCH, LANES), F32),
-            pltpu.VMEM((ITERS, RCH, 1, LANES), F32),
-            pltpu.VMEM((ITERS, NTGT, 1, LANES), F32),
-            pltpu.VMEM((ITERS, RCH, 1, LANES), F32),
+            pltpu.VMEM((ITERS, RCH, LANES), F32),
+            pltpu.VMEM((ITERS, NTGT, RCH, LANES), F32),
             pltpu.VMEM((ITERS, CCH, LANES), F32),
             pltpu.VMEM((ITERS, NSRC, CCH, LANES), F32),
             pltpu.VMEM((CCH, 1, LANES), F32),
@@ -371,7 +362,6 @@
             pltpu.VMEM((2 * OWN, LATENT), F32),
             pltpu.VMEM((MATES, OWN + 8, LATENT), F32),
             pltpu.VMEM((MATES, OWN + 8, LATENT), F32),
-            dma((ITERS, 2)),
             dma((ITERS, 2)),
             dma((ITERS, 2)),
             dma((2,)),
@@ -388,7 +378,7 @@
     )(
         sources,
         targets,
-        log_source.reshape(RCH, 1, LANES),
+        log_source.reshape(RCH, LANES),
         log_target.reshape(CCH, LANES),
     )
     return sp.reshape(ROWS), tp.reshape(COLS), bary

time: 117 us -> 115 us (0.983)
  Pallas kernels: 112 us -> 109 us
    pallas_call x1, Pallas kernels: 112 us -> 109 us  [on_device(): pl.pallas_call(kernel, out_shape=(jax.ShapeDtypeStruct((RCH, LANES), F32)...]
where the time goes in v4:
time: 115 us; the launch traced here: 114 us
  Pallas kernels  109 us (95%)
  local copies, waits for them, and re-layouts  4.22 us (4%)
    pallas_call x1, Pallas kernels, on_device(): pl.pallas_call(kernel, out_shape=(jax.ShapeDtypeStruct((RCH, LANES), F32)...  109 us
    unnamed x7, local copies, waits for them, and re-layouts  4.22 us

profile of v4, /device:TPU:6, one launch (start us, length us, event | category | flops | bytes accessed | tf_op | source)
XLA Modules:
  0.0 114.3 jit_solution(17855981765010618806)
XLA Ops:
  0.6 109.4 %coupling.1 = (f32[16,128]{1,0:T(8,128)}, f32[8,128]{1,0:T(8,128)}, f32[2048,128]{1,0:T(8,128)}) custom-call(f32[2048,128]{1,0:T(8,128)} %x_ref.1, f32[1024,128]{1,0:T(8,128)} %y_ref.1, f32[16,128]{1,0:T(8,128)} %bitcast.6, f32[8,128]{1,0:T(8,128)} %bitcast.7), custom_call_target="tpu_custom_call" | custom-call | flops 6000000000 | bytes 4194304 | tf_op jit(solution)/shard_map/coupling/pallas_call | solution.py:330
  110.0 0.0 copy-start
  110.0 0.7 copy-done
  110.7 0.0 copy-start.1
  110.7 0.6 copy.10
  111.3 0.1 copy-done.1
  111.4 0.6 copy.11
  112.0 2.3 %copy.12 = f32[2048,128]{1,0:T(8,128)} copy(f32[2048,128]{1,0:T(8,128)} %get-tuple-element.14) | data formatting | bytes 2097152
Async XLA Ops:
  110.0 0.7 copy-start
  110.7 0.7 copy-start.1

commit v5 on v4

--- a/solution.py
+++ b/solution.py
@@ -1,3 +1,4 @@
+import functools
 import math
 
 import jax
@@ -19,7 +20,9 @@
 ROWS, COLS = 2048, 1024
 RCH, CCH = ROWS // LANES, COLS // LANES
 OWN = ROWS // NTGT
+O_CHUNKS = 4
 MATES = GRID_X * 2
+DELIVERIES = 8
 PIECE = COLS // MATES
 F32, BF16 = jnp.float32, jnp.bfloat16
 
@@ -38,7 +41,8 @@
     return jnp.broadcast_to(row, (LANES, LANES)).T
 
 
-def lse_pass(z_ref, b_ref, rows, cols, put):
+def lse_down(z_ref, b_ref, top_ref, total_ref):
+    rows, cols = z_ref.shape
     width, depth = 2, 128
 
     @pl.loop(0, cols // (width * LANES))
@@ -56,12 +60,34 @@
             return tuple(out)
 
         start = (jnp.full((8, LANES), -jnp.inf, F32), jnp.zeros((8, LANES), F32))
-        state = lax.fori_loop(0, rows // depth, block, (start,) * width, unroll=4)
+        state = lax.fori_loop(0, rows // depth, block, (start,) * width, unroll=True)
         for k in range(width):
-            top, total = state[k]
-            best = jnp.max(top, axis=0, keepdims=True)
-            total = jnp.sum(total * jnp.exp2(top - best), axis=0, keepdims=True)
-            put(col * width + k, best + LOG2E * jnp.log(total))
+            top_ref[col * width + k], total_ref[col * width + k] = state[k]
+
+    tops = top_ref[...]
+    best = jnp.max(tops, axis=1)
+    total = jnp.sum(total_ref[...] * jnp.exp2(tops - best[:, None, :]), axis=1)
+    return best + LOG2E * jnp.log(total)
+
+
+def lse_across(z_ref, b_ref, top_ref, total_ref, out_ref):
+    rows, cols = z_ref.shape
+    depth = 16
+
+    @pl.loop(0, rows // depth, unroll=4)
+    def _(n):
+        at = pl.ds(pl.multiple_of(n * depth, depth), depth)
+        v = [z_ref[at, c * LANES : (c + 1) * LANES] + b_ref[c : c + 1, :] for c in range(cols // LANES)]
+        top = functools.reduce(jnp.maximum, v)
+        top_ref[at, :] = top
+        total_ref[at, :] = sum(jnp.exp2(x - top) for x in v)
+
+    for k in range(rows // LANES):
+        at = slice(k * LANES, (k + 1) * LANES)
+        top = top_ref[at, :].T
+        best = jnp.max(top, axis=0, keepdims=True)
+        total = jnp.sum(total_ref[at, :].T * jnp.exp2(top - best), axis=0, keepdims=True)
+        out_ref[k : k + 1, :] = best + LOG2E * jnp.log(total)
 
 
 def combine(parts):
@@ -71,7 +97,7 @@
 
 def kernel(
     x_ref, y_ref, la_ref, lb_ref, sp_ref, tp_ref, out_ref,
-    xa, xt, ya, yt, zt, z, qb, pb, nx, ny,
+    xt, ya, zt, zf, qb, pv, nx, ny, top8, total8, tops, totals,
     l_row, rs, l_col, cr, qs, qg, tg, xs, xf, yf, mf, sf, acc, part, shares,
     rs_sem, cr_sem, qg_sem, tr_send, tr_recv, or_send, or_recv, xs_sem, part_sem,
 ):
@@ -106,23 +132,17 @@
     def wait_bytes(ref, sem):
         remote(ref, ref, sem, sem, (s, t)).wait_recv()
 
-    @pl.loop(0, RCH, unroll=2)
+    @pl.loop(0, RCH, unroll=4)
     def _(k):
         at = pl.ds(pl.multiple_of(k * LANES, LANES), LANES)
-        x = x_ref[at, :]
-        turned = x.T
-        nx[pl.ds(k, 1), :] = jnp.sum(turned * turned, axis=0, keepdims=True)
-        xa[at, :] = split3(x * (2.0 * LOG2E), (0, 0, 1))
-        xt[:, at] = split3(turned * (2.0 * LOG2E), (0, 0, 1), axis=0)
-
-    for k in range(CCH):
-        at = slice(k * LANES, (k + 1) * LANES)
+        xt[:, at] = split3(x_ref[at, :].T * (2.0 * LOG2E), (0, 0, 1), axis=0)
+
+    @pl.loop(0, CCH, unroll=2)
+    def _(k):
+        at = pl.ds(pl.multiple_of(k * LANES, LANES), LANES)
         y = y_ref[at, :]
-        turned = y.T
-        ny[k : k + 1, :] = jnp.sum(turned * turned, axis=0, keepdims=True)
         ya[at, :] = split3(y, (0, 1, 0))
-        yt[:, at] = split3(turned, (0, 1, 0), axis=0)
-        qb[at, :] = spread(-LOG2E * ny[k : k + 1, :])
+        qb[at, :] = jnp.broadcast_to(-LOG2E * jnp.sum(y * y, axis=1, keepdims=True), (LANES, LANES))
 
     tg[t] = y_ref[pl.ds(pl.multiple_of(me * PIECE, PIECE), PIECE), :]
     own_rows = pl.ds(pl.multiple_of(t * OWN, OWN), OWN)
@@ -136,10 +156,10 @@
     pl.semaphore_wait(barrier, NTGT - 1 + NSRC - 1)
 
     def hops(way, chunk):
-        return NTGT // 2 - (way ^ chunk)
-
-    def ring_step(view, send, recv, step):
-        for chunk in range(2):
+        return NTGT // 2 - (way ^ chunk % 2)
+
+    def ring_step(view, send, recv, step, chunks=2):
+        for chunk in range(chunks):
             for way in range(2):
                 if step > hops(way, chunk):
                     continue
@@ -164,12 +184,22 @@
         to = mate(lax.rem(me + k, MATES))
         remote(xs.at[me], xs.at[me], xs_sem.at[0], xs_sem.at[1], (to, t)).start()
 
+    def last_scores(first, last):
+        @pl.loop(first, last)
+        def _(b):
+            at = pl.ds(pl.multiple_of(b * 2 * PIECE, 2 * PIECE), 2 * PIECE)
+            y = tg[pl.ds(b * 2, 2)].reshape(2 * PIECE, LATENT)
+            yf[at, :] = split3(y, (0, 1))
+            zf[:, at] = dot(xf[...], split3(y.T, (0, 1, 0), axis=0))
+
+    def last_rows(first, last):
+        @pl.loop(first, last)
+        def _(e):
+            at = pl.ds(pl.multiple_of(e * OWN, OWN), OWN)
+            xf[at, :] = split3(xs[e] * (2.0 * LOG2E), (0, 0, 1))
+
     for it in range(ITERS):
-
-        def put_row(chunk, value):
-            l_row[it, pl.ds(chunk, 1), :] = value
-
-        lse_pass(zt, qb, COLS, ROWS, put_row)
+        l_row[it] = lse_down(zt, qb, top8, total8)
 
         @pl.loop(1, NTGT)
         def _(k):
@@ -178,26 +208,23 @@
         rs[it, t] = l_row[it]
         if it == 0:
             t_step(1)
-            for half in range(2):
-                @pl.loop(half * 2, half * 2 + 2)
-                def _(k):
-                    at = pl.ds(pl.multiple_of(k * 256, 256), 256)
-                    z[:, at] = dot(xa[...], yt[:, at])
-
-                t_step(2 + half)
+            for k in range(RCH):
+                turned = x_ref[k * LANES : (k + 1) * LANES, :].T
+                nx[k : k + 1, :] = jnp.sum(turned * turned, axis=0, keepdims=True)
+            for k in range(CCH):
+                turned = y_ref[k * LANES : (k + 1) * LANES, :].T
+                ny[k : k + 1, :] = jnp.sum(turned * turned, axis=0, keepdims=True)
+            t_step(2)
         else:
-            t_step(7)
+            t_step(8)
+            last_scores(0, NTGT // 4)
 
         wait_bytes(rs.at[it, pl.ds(0, NTGT - 1)], rs_sem.at[it, 1])
         row_pot = LOG2E * la_ref[...] - combine(rs[it])
-        for k in range(RCH):
-            pb[k * LANES : (k + 1) * LANES, :] = spread(row_pot[k : k + 1, :])
-        t_step(4 if it == 0 else 8)
-
-        def put_col(chunk, value):
-            l_col[it, pl.ds(chunk, 1), :] = value
-
-        lse_pass(z, pb, ROWS, COLS, put_col)
+        pv[...] = row_pot
+        if it == 0:
+            t_step(3)
+        lse_across(zt, pv, tops, totals, l_col.at[it])
 
         @pl.loop(1, NSRC)
         def _(k):
@@ -205,29 +232,22 @@
 
         cr[it, s] = l_col[it]
         if it == 0:
+            t_step(4)
+            wait_bytes(xs.at[pl.ds(0, MATES - 1)], xs_sem.at[1])
+            last_rows(0, MATES // 2)
             t_step(5)
+            last_rows(MATES // 2, MATES)
+            t_step(6)
         else:
             sp_ref[...] = row_pot * LN2 + nx[...]
-            wait_bytes(xs.at[pl.ds(0, MATES - 1)], xs_sem.at[1])
-
-            @pl.loop(0, MATES)
-            def _(e):
-                at = pl.ds(pl.multiple_of(e * OWN, OWN), OWN)
-                xf[at, :] = split3(xs[e] * (2.0 * LOG2E), (0, 0, 1))
-
-            @pl.loop(0, NTGT // 2)
-            def _(b):
-                at = pl.ds(pl.multiple_of(b * 2 * PIECE, 2 * PIECE), 2 * PIECE)
-                y = tg[pl.ds(b * 2, 2)].reshape(2 * PIECE, LATENT)
-                yf[at, :] = split3(y, (0, 1))
-                zt[:, at] = dot(xf[...], split3(y.T, (0, 1, 0), axis=0))
+            last_scores(NTGT // 4, NTGT // 2)
 
         wait_bytes(cr.at[it, pl.ds(0, NSRC - 1)], cr_sem.at[it, 1])
         q = LOG2E * lb_ref[...] - combine(cr[it])
         if it == 0:
             for k in range(CCH):
                 qb[k * LANES : (k + 1) * LANES, :] = spread(q[k : k + 1, :])
-            t_step(6)
+            t_step(7)
 
     for k in range(CCH):
         qs[k] = q[k : k + 1, :]
@@ -248,9 +268,9 @@
         @pl.loop(0, 2 * OWN // depth)
         def _(r):
             at = pl.ds(pl.multiple_of(base + r * depth, depth), depth)
-            best = zt[at, 0:LANES] + qg[0]
+            best = zf[at, 0:LANES] + qg[0]
             for b in range(1, NTGT):
-                best = jnp.maximum(best, zt[at, b * LANES : (b + 1) * LANES] + qg[b])
+                best = jnp.maximum(best, zf[at, b * LANES : (b + 1) * LANES] + qg[b])
             to = pl.ds(pl.multiple_of(r * depth, depth), depth)
             mf[to, :] = jnp.broadcast_to(jnp.max(best, axis=1, keepdims=True), (depth, LANES))
 
@@ -259,13 +279,13 @@
         at = pl.ds(pl.multiple_of(base, 2 * OWN), 2 * OWN)
         group = 4
 
-        @pl.loop(0, NTGT // group)
+        @pl.loop(0, NTGT // group, unroll=2)
         def _(b):
             highs, lows = [], []
             total = sf[...]
             for k in range(group):
                 lane = pl.ds(pl.multiple_of((b * group + k) * LANES, LANES), LANES)
-                w = jnp.exp2(zt[at, lane] + qg[b * group + k] - mf[...])
+                w = jnp.exp2(zf[at, lane] + qg[b * group + k] - mf[...])
                 total += w
                 high = w.astype(BF16)
                 highs.append(high)
@@ -305,23 +325,38 @@
     out_ref[own_rows, :] = out
 
     def o_view(chunk, block):
-        rows = OWN // 2
+        rows = OWN // O_CHUNKS
         return out_ref.at[pl.ds(pl.multiple_of(block * OWN + chunk * rows, rows), rows), :]
 
     for step in range(NTGT // 2 + 1):
-        ring_step(o_view, or_send, or_recv, step)
+        ring_step(o_view, or_send, or_recv, step, O_CHUNKS)
 
     for chunk in range(2):
         for way in range(2):
             n = hops(way, chunk)
             wait_bytes(tg.at[pl.ds(0, n), pl.ds(0, PIECE // 2), :], tr_send.at[way, chunk])
-            wait_bytes(out_ref.at[pl.ds(0, n * (OWN // 2)), :], or_send.at[way, chunk])
+    for chunk in range(O_CHUNKS):
+        for way in range(2):
+            wait_bytes(out_ref.at[pl.ds(0, hops(way, chunk) * (OWN // O_CHUNKS)), :], or_send.at[way, chunk])
     wait_bytes(xs.at[pl.ds(0, MATES - 1)], xs_sem.at[0])
     wait_bytes(part.at[pl.ds(0, MATES - 1)], part_sem.at[0])
     for it in range(ITERS):
         wait_bytes(rs.at[it, pl.ds(0, NTGT - 1)], rs_sem.at[it, 0])
         wait_bytes(cr.at[it, pl.ds(0, NSRC - 1)], cr_sem.at[it, 0])
     wait_bytes(qg.at[pl.ds(0, NTGT - 1)], qg_sem.at[0])
+
+
+def deliver(sp_in, tp_in, bary_in, sp_out, tp_out, bary_out, sems):
+    rows = ROWS // DELIVERIES
+    copies = [(sp_in, sp_out), (tp_in, tp_out)]
+    for k in range(DELIVERIES):
+        at = pl.ds(k * rows, rows)
+        copies.append((bary_in.at[at, :], bary_out.at[at, :]))
+    copies = [pltpu.make_async_copy(a, b, sems.at[k]) for k, (a, b) in enumerate(copies)]
+    for copy in copies:
+        copy.start()
+    for copy in copies:
+        copy.wait()
 
 
 def on_device(sources, targets, log_source, log_target):
@@ -337,16 +372,18 @@
         in_specs=[vmem] * 4,
         out_specs=(vmem,) * 3,
         scratch_shapes=[
-            pltpu.VMEM((ROWS, 3 * LATENT), BF16),
             pltpu.VMEM((3 * LATENT, ROWS), BF16),
             pltpu.VMEM((COLS, 3 * LATENT), BF16),
-            pltpu.VMEM((3 * LATENT, COLS), BF16),
             pltpu.VMEM((COLS, ROWS), F32),
-            pltpu.VMEM((ROWS, COLS), F32),
+            pltpu.VMEM((MATES * OWN, NTGT * PIECE), F32),
             pltpu.VMEM((COLS, LANES), F32),
-            pltpu.VMEM((ROWS, LANES), F32),
+            pltpu.VMEM((RCH, LANES), F32),
             pltpu.VMEM((RCH, LANES), F32),
             pltpu.VMEM((CCH, LANES), F32),
+            pltpu.VMEM((RCH, 8, LANES), F32),
+            pltpu.VMEM((RCH, 8, LANES), F32),
+            pltpu.VMEM((COLS, LANES), F32),
+            pltpu.VMEM((COLS, LANES), F32),
             pltpu.VMEM((ITERS, RCH, LANES), F32),
             pltpu.VMEM((ITERS, NTGT, RCH, LANES), F32),
             pltpu.VMEM((ITERS, CCH, LANES), F32),
@@ -366,7 +403,7 @@
             dma((ITERS, 2)),
             dma((2,)),
             dma((2, 2)), dma((2, 2, 8)),
-            dma((2, 2)), dma((2, 2, 8)),
+            dma((2, O_CHUNKS)), dma((2, O_CHUNKS, 8)),
             dma((2,)),
             dma((2,)),
         ],
@@ -381,6 +418,14 @@
         log_source.reshape(RCH, LANES),
         log_target.reshape(CCH, LANES),
     )
+    sp, tp, bary = pl.pallas_call(
+        deliver,
+        out_shape=tuple(jax.ShapeDtypeStruct(v.shape, F32) for v in (sp, tp, bary)),
+        in_specs=[pl.BlockSpec(memory_space=pl.ANY)] * 3,
+        out_specs=(pl.BlockSpec(memory_space=pl.ANY),) * 3,
+        scratch_shapes=[dma((2 + DELIVERIES,))],
+        name="deliver",
+    )(sp, tp, bary)
     return sp.reshape(ROWS), tp.reshape(COLS), bary
 
 

time: 115 us -> 142 us (1.23)
  Pallas kernels: 109 us -> 142 us
  local copies, waits for them, and re-layouts: 4.22 us -> 0 us
    pallas_call x0 -> x1, Pallas kernels: none -> 33.3 us  [on_device(): pl.pallas_call(deliver, out_shape=tuple((jax.ShapeDtypeStruct(v.shape, F3...]
    unnamed x7 -> x0, local copies, waits for them, and re-layouts: 4.22 us -> none
where the time goes in v5:
time: 142 us
  Pallas kernels  142 us (100%)
    pallas_call x1, Pallas kernels, on_device(): pl.pallas_call(kernel, out_shape=(jax.ShapeDtypeStruct((RCH, LANES), F32)...  108 us
    pallas_call x1, Pallas kernels, on_device(): pl.pallas_call(deliver, out_shape=tuple((jax.ShapeDtypeStruct(v.shape, F3...  33.3 us

profile of v5, /device:TPU:6, one launch (start us, length us, event | category | flops | bytes accessed | tf_op | source)
XLA Modules:
  0.0 142.2 jit_solution(4444105506614335481)
XLA Ops:
  0.6 108.2 %coupling.1 = (f32[16,128]{1,0:T(8,128)}, f32[8,128]{1,0:T(8,128)}, f32[2048,128]{1,0:T(8,128)}) custom-call(f32[2048,128]{1,0:T(8,128)} %x_ref.1, f32[1024,128]{1,0:T(8,128)} %y_ref.1, f32[16,128]{1,0:T(8,128)} %bitcast.4, f32[8,128]{1,0:T(8,128)} %bitcast.6), custom_call_target="tpu_custom_call" | custom-call | flops 6000000000 | bytes 4194304 | tf_op jit(solution)/shard_map/coupling/pallas_call | solution.py:365
  108.8 33.3 %deliver.1 = (f32[16,128]{1,0:T(8,128)}, f32[8,128]{1,0:T(8,128)}, f32[2048,128]{1,0:T(8,128)}) custom-call(f32[16,128]{1,0:T(8,128)} %get-tuple-element.9.sp_in, f32[8,128]{1,0:T(8,128)} %get-tuple-element.10.tp_in, f32[2048,128]{1,0:T(8,128)} %get-tuple-element.11.bary_in), custom_call_target="tpu_custom_call" | custom-call | tf_op jit(solution)/shard_map/deliver/pallas_call | solution.py:421

commit v6 on v5

--- a/solution.py
+++ b/solution.py
@@ -20,9 +20,7 @@
 ROWS, COLS = 2048, 1024
 RCH, CCH = ROWS // LANES, COLS // LANES
 OWN = ROWS // NTGT
-O_CHUNKS = 4
 MATES = GRID_X * 2
-DELIVERIES = 8
 PIECE = COLS // MATES
 F32, BF16 = jnp.float32, jnp.bfloat16
 
@@ -99,7 +97,7 @@
     x_ref, y_ref, la_ref, lb_ref, sp_ref, tp_ref, out_ref,
     xt, ya, zt, zf, qb, pv, nx, ny, top8, total8, tops, totals,
     l_row, rs, l_col, cr, qs, qg, tg, xs, xf, yf, mf, sf, acc, part, shares,
-    rs_sem, cr_sem, qg_sem, tr_send, tr_recv, or_send, or_recv, xs_sem, part_sem,
+    rs_sem, cr_sem, qg_sem, tr_send, tr_recv, xs_sem, part_sem,
 ):
     s, t = lax.axis_index("src"), lax.axis_index("tgt")
     gx, gy, core = s // (GRID_Y * 2), lax.rem(s // 2, GRID_Y), lax.rem(s, 2)
@@ -322,41 +320,18 @@
     out = jnp.zeros((OWN, LATENT), F32)
     for e in range(MATES):
         out += spread(scales[e] / total) * shares[e, 0:OWN, :]
-    out_ref[own_rows, :] = out
-
-    def o_view(chunk, block):
-        rows = OWN // O_CHUNKS
-        return out_ref.at[pl.ds(pl.multiple_of(block * OWN + chunk * rows, rows), rows), :]
-
-    for step in range(NTGT // 2 + 1):
-        ring_step(o_view, or_send, or_recv, step, O_CHUNKS)
+    out_ref[...] = out
 
     for chunk in range(2):
         for way in range(2):
             n = hops(way, chunk)
             wait_bytes(tg.at[pl.ds(0, n), pl.ds(0, PIECE // 2), :], tr_send.at[way, chunk])
-    for chunk in range(O_CHUNKS):
-        for way in range(2):
-            wait_bytes(out_ref.at[pl.ds(0, hops(way, chunk) * (OWN // O_CHUNKS)), :], or_send.at[way, chunk])
     wait_bytes(xs.at[pl.ds(0, MATES - 1)], xs_sem.at[0])
     wait_bytes(part.at[pl.ds(0, MATES - 1)], part_sem.at[0])
     for it in range(ITERS):
         wait_bytes(rs.at[it, pl.ds(0, NTGT - 1)], rs_sem.at[it, 0])
         wait_bytes(cr.at[it, pl.ds(0, NSRC - 1)], cr_sem.at[it, 0])
     wait_bytes(qg.at[pl.ds(0, NTGT - 1)], qg_sem.at[0])
-
-
-def deliver(sp_in, tp_in, bary_in, sp_out, tp_out, bary_out, sems):
-    rows = ROWS // DELIVERIES
-    copies = [(sp_in, sp_out), (tp_in, tp_out)]
-    for k in range(DELIVERIES):
-        at = pl.ds(k * rows, rows)
-        copies.append((bary_in.at[at, :], bary_out.at[at, :]))
-    copies = [pltpu.make_async_copy(a, b, sems.at[k]) for k, (a, b) in enumerate(copies)]
-    for copy in copies:
-        copy.start()
-    for copy in copies:
-        copy.wait()
 
 
 def on_device(sources, targets, log_source, log_target):
@@ -367,7 +342,7 @@
         out_shape=(
             jax.ShapeDtypeStruct((RCH, LANES), F32),
             jax.ShapeDtypeStruct((CCH, LANES), F32),
-            jax.ShapeDtypeStruct((ROWS, LATENT), F32),
+            jax.ShapeDtypeStruct((OWN, LATENT), F32),
         ),
         in_specs=[vmem] * 4,
         out_specs=(vmem,) * 3,
@@ -403,7 +378,6 @@
             dma((ITERS, 2)),
             dma((2,)),
             dma((2, 2)), dma((2, 2, 8)),
-            dma((2, O_CHUNKS)), dma((2, O_CHUNKS, 8)),
             dma((2,)),
             dma((2,)),
         ],
@@ -418,14 +392,7 @@
         log_source.reshape(RCH, LANES),
         log_target.reshape(CCH, LANES),
     )
-    sp, tp, bary = pl.pallas_call(
-        deliver,
-        out_shape=tuple(jax.ShapeDtypeStruct(v.shape, F32) for v in (sp, tp, bary)),
-        in_specs=[pl.BlockSpec(memory_space=pl.ANY)] * 3,
-        out_specs=(pl.BlockSpec(memory_space=pl.ANY),) * 3,
-        scratch_shapes=[dma((2 + DELIVERIES,))],
-        name="deliver",
-    )(sp, tp, bary)
+    bary = lax.all_gather(bary, "tgt", axis=0, tiled=True)
     return sp.reshape(ROWS), tp.reshape(COLS), bary
 
 

time: 142 us -> 164 us (1.15)
  waiting for transfers between devices: 0 us -> 65.7 us
  Pallas kernels: 142 us -> 80.8 us
  between operations: 0.64 us -> 14.1 us
  local copies, waits for them, and re-layouts: 0 us -> 3.46 us
    all_gather x0 -> x1, waiting for transfers between devices: none -> 65.7 us  [on_device(): bary = lax.all_gather(bary, 'tgt', axis=0, tiled=True)]
    pallas_call x1 -> x0, Pallas kernels: 33.3 us -> none  [on_device(): pl.pallas_call(deliver, out_shape=tuple((jax.ShapeDtypeStruct(v.shape, F3...]
    pallas_call x1, Pallas kernels: 108 us -> 80.8 us  [on_device(): pl.pallas_call(kernel, out_shape=(jax.ShapeDtypeStruct((RCH, LANES), F32)...]
    unnamed x0 -> x7, local copies, waits for them, and re-layouts: none -> 3.46 us
  transfers between devices with their start and end apart: 0 -> 1, of which waited for: 0 -> 1; matrix products, arithmetic and copies ran while one was open for 0% -> 0% of each run, Pallas kernels for 0% -> 0%
where the time goes in v6:
time: 164 us
  Pallas kernels  80.8 us (49%)
  waiting for transfers between devices  65.7 us (40%)
  between operations  14.1 us (9%)
  local copies, waits for them, and re-layouts  3.46 us (2%)
    pallas_call x1, Pallas kernels, on_device(): pl.pallas_call(kernel, out_shape=(jax.ShapeDtypeStruct((RCH, LANES), F32)...  80.8 us
    all_gather x1, waiting for transfers between devices, on_device(): bary = lax.all_gather(bary, 'tgt', axis=0, tiled=True)  65.7 us
    unnamed x7, local copies, waits for them, and re-layouts  3.46 us
  transfers between devices with their start and end apart: 1, of which 1 were waited for; matrix products, arithmetic and copies ran while one was open for 0% of the time, Pallas kernels for 0%

profile of v6, /device:TPU:6, one launch (start us, length us, event | category | flops | bytes accessed | tf_op | source)
XLA Modules:
  0.0 164.0 jit_solution(6148602511703450382)
XLA Ops:
  7.2 0.0 all-gather.2.cloned.1.call-start
  7.2 80.8 %coupling.1 = (f32[16,128]{1,0:T(8,128)}, f32[8,128]{1,0:T(8,128)}, f32[128,128]{1,0:T(8,128)}) custom-call(f32[2048,128]{1,0:T(8,128)} %x_ref.1, f32[1024,128]{1,0:T(8,128)} %y_ref.1, f32[16,128]{1,0:T(8,128)} %bitcast.6, f32[8,128]{1,0:T(8,128)} %bitcast.7), custom_call_target="tpu_custom_call" | custom-call | flops 6000000000 | bytes 4194304 | tf_op jit(solution)/shard_map/coupling/pallas_call | solution.py:340
  88.0 0.0 copy-start
  88.0 0.0 all-gather.2.cloned.1.call-update
  88.0 0.0 copy-start.1
  88.1 65.7 %all-gather.2.cloned.1.call-done = f32[2048,128]{1,0:T(8,128)} async-done(((f32[128,128]{1,0:T(8,128)}), f32[2048,128]{1,0:T(8,128)}) %all-gather.2.cloned.1.call-update) | async-done | bytes 1048592 | tf_op jit(solution)/shard_map/all_gather | solution.py:395
  153.7 0.0 copy-done
  153.7 0.6 copy.10
  154.3 0.0 copy-done.1
  154.3 0.6 copy.11
  154.9 2.3 %copy.12 = f32[2048,128]{1,0:T(8,128)} copy(f32[2048,128]{1,0:T(8,128)} %all-gather.2.cloned.1.call-done) | data formatting | bytes 2097152
Async XLA Ops:
  7.2 146.6 %all-gather.2.cloned.1.call-start = ((), (), s32[]{:S(2)}) async-start(), calls=%async_computation | async-start | bytes 1114112 | tf_op jit(solution)/shard_map/all_gather | solution.py:395
  88.0 65.7 %copy-start = (f32[16,128]{1,0:T(8,128)S(1)}, f32[16,128]{1,0:T(8,128)}, u32[]{:S(2)}) copy-start(f32[16,128]{1,0:T(8,128)} %get-tuple-element.6) | copy-start | bytes 24580
  88.0 66.3 %copy-start.1 = (f32[8,128]{1,0:T(8,128)S(1)}, f32[8,128]{1,0:T(8,128)}, u32[]{:S(2)}) copy-start(f32[8,128]{1,0:T(8,128)} %get-tuple-element.7) | copy-start | bytes 12292
Sparse Core Ops, SparseCore 0:
  88.2 65.5 all-gather.1

commit v7 on v6

--- a/solution.py
+++ b/solution.py
@@ -20,7 +20,9 @@
 ROWS, COLS = 2048, 1024
 RCH, CCH = ROWS // LANES, COLS // LANES
 OWN = ROWS // NTGT
+O_CHUNKS = 2
 MATES = GRID_X * 2
+DELIVERIES = 4
 PIECE = COLS // MATES
 F32, BF16 = jnp.float32, jnp.bfloat16
 
@@ -97,7 +99,7 @@
     x_ref, y_ref, la_ref, lb_ref, sp_ref, tp_ref, out_ref,
     xt, ya, zt, zf, qb, pv, nx, ny, top8, total8, tops, totals,
     l_row, rs, l_col, cr, qs, qg, tg, xs, xf, yf, mf, sf, acc, part, shares,
-    rs_sem, cr_sem, qg_sem, tr_send, tr_recv, xs_sem, part_sem,
+    rs_sem, cr_sem, qg_sem, tr_send, tr_recv, or_send, or_recv, xs_sem, part_sem,
 ):
     s, t = lax.axis_index("src"), lax.axis_index("tgt")
     gx, gy, core = s // (GRID_Y * 2), lax.rem(s // 2, GRID_Y), lax.rem(s, 2)
@@ -153,21 +155,34 @@
 
     pl.semaphore_wait(barrier, NTGT - 1 + NSRC - 1)
 
-    def hops(way, chunk):
+    def reach(way, chunk):
         return NTGT // 2 - (way ^ chunk % 2)
 
-    def ring_step(view, send, recv, step, chunks=2):
+    def away(way, distance):
+        return lax.rem(t + (distance if way == 0 else NTGT - distance), NTGT)
+
+    def ring_wait(view, recv, way, chunk, distance):
+        ref = view(chunk, away(1 - way, distance))
+        wait_bytes(ref, recv.at[way, chunk, distance - 1])
+
+    def ring_step(view, send, recv, distance, chunks=2):
         for chunk in range(chunks):
             for way in range(2):
-                if step > hops(way, chunk):
-                    continue
-                block = lax.rem(t + (NTGT - step if way == 0 else step), NTGT)
-                ref = view(chunk, block)
-                if step > 0:
-                    wait_bytes(ref, recv.at[way, chunk, step - 1])
-                if step < hops(way, chunk):
-                    to = lax.rem(t + (1 if way == 0 else NTGT - 1), NTGT)
-                    remote(ref, ref, send.at[way, chunk], recv.at[way, chunk, step], (s, to)).start()
+                if distance > 0:
+                    ring_wait(view, recv, way, chunk, distance)
+                ref = view(chunk, away(1 - way, distance))
+                for stride in (2, 1):
+                    there = distance + stride
+                    if there <= reach(way, chunk):
+                        at = recv.at[way, chunk, there - 1]
+                        remote(ref, ref, send.at[way, chunk], at, (s, away(way, stride))).start()
+
+    def ring_end(view, recv, chunks=2):
+        for distance in (1, 3, 5, 7, 8):
+            for chunk in range(chunks):
+                for way in range(2):
+                    if distance <= reach(way, chunk):
+                        ring_wait(view, recv, way, chunk, distance)
 
     def t_view(chunk, block):
         return tg.at[block, pl.ds(chunk * (PIECE // 2), PIECE // 2), :]
@@ -205,23 +220,22 @@
 
         rs[it, t] = l_row[it]
         if it == 0:
-            t_step(1)
+            t_step(2)
             for k in range(RCH):
                 turned = x_ref[k * LANES : (k + 1) * LANES, :].T
                 nx[k : k + 1, :] = jnp.sum(turned * turned, axis=0, keepdims=True)
             for k in range(CCH):
                 turned = y_ref[k * LANES : (k + 1) * LANES, :].T
                 ny[k : k + 1, :] = jnp.sum(turned * turned, axis=0, keepdims=True)
-            t_step(2)
         else:
-            t_step(8)
+            ring_end(t_view, tr_recv)
             last_scores(0, NTGT // 4)
 
         wait_bytes(rs.at[it, pl.ds(0, NTGT - 1)], rs_sem.at[it, 1])
         row_pot = LOG2E * la_ref[...] - combine(rs[it])
         pv[...] = row_pot
         if it == 0:
-            t_step(3)
+            t_step(4)
         lse_across(zt, pv, tops, totals, l_col.at[it])
 
         @pl.loop(1, NSRC)
@@ -230,11 +244,8 @@
 
         cr[it, s] = l_col[it]
         if it == 0:
-            t_step(4)
             wait_bytes(xs.at[pl.ds(0, MATES - 1)], xs_sem.at[1])
-            last_rows(0, MATES // 2)
-            t_step(5)
-            last_rows(MATES // 2, MATES)
+            last_rows(0, MATES)
             t_step(6)
         else:
             sp_ref[...] = row_pot * LN2 + nx[...]
@@ -245,7 +256,6 @@
         if it == 0:
             for k in range(CCH):
                 qb[k * LANES : (k + 1) * LANES, :] = spread(q[k : k + 1, :])
-            t_step(7)
 
     for k in range(CCH):
         qs[k] = q[k : k + 1, :]
@@ -320,18 +330,35 @@
     out = jnp.zeros((OWN, LATENT), F32)
     for e in range(MATES):
         out += spread(scales[e] / total) * shares[e, 0:OWN, :]
-    out_ref[...] = out
+    out_ref[own_rows, :] = out
+
+    def o_view(chunk, block):
+        rows = OWN // O_CHUNKS
+        return out_ref.at[pl.ds(pl.multiple_of(block * OWN + chunk * rows, rows), rows), :]
+
+    for distance in range(0, NTGT // 2, 2):
+        ring_step(o_view, or_send, or_recv, distance, O_CHUNKS)
+    ring_end(o_view, or_recv, O_CHUNKS)
 
     for chunk in range(2):
         for way in range(2):
-            n = hops(way, chunk)
+            n = reach(way, chunk)
             wait_bytes(tg.at[pl.ds(0, n), pl.ds(0, PIECE // 2), :], tr_send.at[way, chunk])
+    for chunk in range(O_CHUNKS):
+        for way in range(2):
+            wait_bytes(out_ref.at[pl.ds(0, reach(way, chunk) * (OWN // O_CHUNKS)), :], or_send.at[way, chunk])
     wait_bytes(xs.at[pl.ds(0, MATES - 1)], xs_sem.at[0])
     wait_bytes(part.at[pl.ds(0, MATES - 1)], part_sem.at[0])
     for it in range(ITERS):
         wait_bytes(rs.at[it, pl.ds(0, NTGT - 1)], rs_sem.at[it, 0])
         wait_bytes(cr.at[it, pl.ds(0, NSRC - 1)], cr_sem.at[it, 0])
     wait_bytes(qg.at[pl.ds(0, NTGT - 1)], qg_sem.at[0])
+
+
+def deliver(sp_in, tp_in, bary_in, sp_out, tp_out, bary_out):
+    sp_out[...] = sp_in[...]
+    tp_out[...] = tp_in[...]
+    bary_out[...] = bary_in[...]
 
 
 def on_device(sources, targets, log_source, log_target):
@@ -342,7 +369,7 @@
         out_shape=(
             jax.ShapeDtypeStruct((RCH, LANES), F32),
             jax.ShapeDtypeStruct((CCH, LANES), F32),
-            jax.ShapeDtypeStruct((OWN, LATENT), F32),
+            jax.ShapeDtypeStruct((ROWS, LATENT), F32),
         ),
         in_specs=[vmem] * 4,
         out_specs=(vmem,) * 3,
@@ -378,6 +405,7 @@
             dma((ITERS, 2)),
             dma((2,)),
             dma((2, 2)), dma((2, 2, 8)),
+            dma((2, O_CHUNKS)), dma((2, O_CHUNKS, 8)),
             dma((2,)),
             dma((2,)),
         ],
@@ -392,7 +420,19 @@
         log_source.reshape(RCH, LANES),
         log_target.reshape(CCH, LANES),
     )
-    bary = lax.all_gather(bary, "tgt", axis=0, tiled=True)
+    blocks = [
+        pl.BlockSpec((RCH, LANES), lambda k: (0, 0)),
+        pl.BlockSpec((CCH, LANES), lambda k: (0, 0)),
+        pl.BlockSpec((ROWS // DELIVERIES, LATENT), lambda k: (k, 0)),
+    ]
+    sp, tp, bary = pl.pallas_call(
+        deliver,
+        out_shape=tuple(jax.ShapeDtypeStruct(v.shape, F32) for v in (sp, tp, bary)),
+        grid=(DELIVERIES,),
+        in_specs=blocks,
+        out_specs=tuple(blocks),
+        name="deliver",
+    )(sp, tp, bary)
     return sp.reshape(ROWS), tp.reshape(COLS), bary
 
 

time: 164 us -> 105 us (0.64); the launches traced: 164 us -> 103 us
  waiting for transfers between devices: 65.7 us -> 0 us
  Pallas kernels: 80.8 us -> 102 us
  between operations: 14.1 us -> 0.64 us
  local copies, waits for them, and re-layouts: 3.46 us -> 0 us
    all_gather x1 -> x0, waiting for transfers between devices: 65.7 us -> none  [on_device(): bary = lax.all_gather(bary, 'tgt', axis=0, tiled=True)]
    pallas_call x1, Pallas kernels: 80.8 us -> 98.6 us  [on_device(): pl.pallas_call(kernel, out_shape=(jax.ShapeDtypeStruct((RCH, LANES), F32)...]
    unnamed x7 -> x0, local copies, waits for them, and re-layouts: 3.46 us -> none
    pallas_call x0 -> x1, Pallas kernels: none -> 3.38 us  [on_device(): pl.pallas_call(deliver, out_shape=tuple((jax.ShapeDtypeStruct(v.shape, F3...]
  transfers between devices with their start and end apart: 1 -> 0, of which waited for: 1 -> 0; matrix products, arithmetic and copies ran while one was open for 0% -> 0% of each run, Pallas kernels for 0% -> 0%
where the time goes in v7:
time: 105 us; the launch traced here: 103 us
  Pallas kernels  102 us (97%)
    pallas_call x1, Pallas kernels, on_device(): pl.pallas_call(kernel, out_shape=(jax.ShapeDtypeStruct((RCH, LANES), F32)...  98.6 us
    pallas_call x1, Pallas kernels, on_device(): pl.pallas_call(deliver, out_shape=tuple((jax.ShapeDtypeStruct(v.shape, F3...  3.38 us

profile of v7, /device:TPU:6, one launch (start us, length us, event | category | flops | bytes accessed | tf_op | source)
XLA Modules:
  0.0 102.6 jit_solution(3046370051486378955)
XLA Ops:
  0.6 98.6 %coupling.1 = (f32[16,128]{1,0:T(8,128)}, f32[8,128]{1,0:T(8,128)}, f32[2048,128]{1,0:T(8,128)}) custom-call(f32[2048,128]{1,0:T(8,128)} %x_ref.1, f32[1024,128]{1,0:T(8,128)} %y_ref.1, f32[16,128]{1,0:T(8,128)} %bitcast.4, f32[8,128]{1,0:T(8,128)} %bitcast.6), custom_call_target="tpu_custom_call" | custom-call | flops 6000000000 | bytes 4194304 | tf_op jit(solution)/shard_map/coupling/pallas_call | solution.py:367
  99.2 3.4 %deliver.1 = (f32[16,128]{1,0:T(8,128)}, f32[8,128]{1,0:T(8,128)}, f32[2048,128]{1,0:T(8,128)}) custom-call(f32[16,128]{1,0:T(8,128)} %get-tuple-element.9.sp_in, f32[8,128]{1,0:T(8,128)} %get-tuple-element.10.tp_in, f32[2048,128]{1,0:T(8,128)} %get-tuple-element.11.bary_in), custom_call_target="tpu_custom_call" | custom-call | tf_op jit(solution)/shard_map/deliver/pallas_call | solution.py:428

commit v8 on v7

--- a/solution.py
+++ b/solution.py
@@ -220,7 +220,6 @@
 
         rs[it, t] = l_row[it]
         if it == 0:
-            t_step(2)
             for k in range(RCH):
                 turned = x_ref[k * LANES : (k + 1) * LANES, :].T
                 nx[k : k + 1, :] = jnp.sum(turned * turned, axis=0, keepdims=True)
@@ -234,8 +233,6 @@
         wait_bytes(rs.at[it, pl.ds(0, NTGT - 1)], rs_sem.at[it, 1])
         row_pot = LOG2E * la_ref[...] - combine(rs[it])
         pv[...] = row_pot
-        if it == 0:
-            t_step(4)
         lse_across(zt, pv, tops, totals, l_col.at[it])
 
         @pl.loop(1, NSRC)
@@ -244,9 +241,10 @@
 
         cr[it, s] = l_col[it]
         if it == 0:
+            t_step(2)
             wait_bytes(xs.at[pl.ds(0, MATES - 1)], xs_sem.at[1])
             last_rows(0, MATES)
-            t_step(6)
+            t_step(4)
         else:
             sp_ref[...] = row_pot * LN2 + nx[...]
             last_scores(NTGT // 4, NTGT // 2)
@@ -256,6 +254,7 @@
         if it == 0:
             for k in range(CCH):
                 qb[k * LANES : (k + 1) * LANES, :] = spread(q[k : k + 1, :])
+            t_step(6)
 
     for k in range(CCH):
         qs[k] = q[k : k + 1, :]
@@ -355,10 +354,21 @@
     wait_bytes(qg.at[pl.ds(0, NTGT - 1)], qg_sem.at[0])
 
 
-def deliver(sp_in, tp_in, bary_in, sp_out, tp_out, bary_out):
-    sp_out[...] = sp_in[...]
-    tp_out[...] = tp_in[...]
-    bary_out[...] = bary_in[...]
+def deliver(sp_in, tp_in, bary_in, sp_out, tp_out, bary_out, sp_v, tp_v, bary_v, in_sems, out_sems):
+    parts = [(sp_in, sp_v, sp_out), (tp_in, tp_v, tp_out)]
+    rows = ROWS // DELIVERIES
+    for k in range(DELIVERIES):
+        at = pl.ds(k * rows, rows)
+        parts.append((bary_in.at[at, :], bary_v.at[at, :], bary_out.at[at, :]))
+    ins = [pltpu.make_async_copy(a, v, in_sems.at[k]) for k, (a, v, _) in enumerate(parts)]
+    outs = [pltpu.make_async_copy(v, b, out_sems.at[k]) for k, (_, v, b) in enumerate(parts)]
+    for copy in ins:
+        copy.start()
+    for first, second in zip(ins, outs):
+        first.wait()
+        second.start()
+    for copy in outs:
+        copy.wait()
 
 
 def on_device(sources, targets, log_source, log_target):
@@ -420,17 +430,18 @@
         log_source.reshape(RCH, LANES),
         log_target.reshape(CCH, LANES),
     )
-    blocks = [
-        pl.BlockSpec((RCH, LANES), lambda k: (0, 0)),
-        pl.BlockSpec((CCH, LANES), lambda k: (0, 0)),
-        pl.BlockSpec((ROWS // DELIVERIES, LATENT), lambda k: (k, 0)),
-    ]
     sp, tp, bary = pl.pallas_call(
         deliver,
         out_shape=tuple(jax.ShapeDtypeStruct(v.shape, F32) for v in (sp, tp, bary)),
-        grid=(DELIVERIES,),
-        in_specs=blocks,
-        out_specs=tuple(blocks),
+        in_specs=[pl.BlockSpec(memory_space=pl.ANY)] * 3,
+        out_specs=(pl.BlockSpec(memory_space=pl.ANY),) * 3,
+        scratch_shapes=[
+            pltpu.VMEM((RCH, LANES), F32),
+            pltpu.VMEM((CCH, LANES), F32),
+            pltpu.VMEM((ROWS, LATENT), F32),
+            dma((2 + DELIVERIES,)),
+            dma((2 + DELIVERIES,)),
+        ],
         name="deliver",
     )(sp, tp, bary)
     return sp.reshape(ROWS), tp.reshape(COLS), bary

time: 105 us -> 104 us (level); the launches traced: 103 us -> 103 us
    pallas_call x1, Pallas kernels: 98.6 us -> 101 us  [on_device(): pl.pallas_call(kernel, out_shape=(jax.ShapeDtypeStruct((RCH, LANES), F32)...]
    pallas_call x1, Pallas kernels: 3.38 us -> 2.04 us  [on_device(): pl.pallas_call(deliver, out_shape=tuple((jax.ShapeDtypeStruct(v.shape, F3...]
where the time goes in v8:
time: 104 us; the launch traced here: 103 us
  Pallas kernels  103 us (99%)
    pallas_call x1, Pallas kernels, on_device(): pl.pallas_call(kernel, out_shape=(jax.ShapeDtypeStruct((RCH, LANES), F32)...  101 us

profile of v8, /device:TPU:6, one launch (start us, length us, event | category | flops | bytes accessed | tf_op | source)
XLA Modules:
  0.0 103.5 jit_solution(13224093798509011859)
XLA Ops:
  0.6 100.8 %coupling.1 = (f32[16,128]{1,0:T(8,128)}, f32[8,128]{1,0:T(8,128)}, f32[2048,128]{1,0:T(8,128)}) custom-call(f32[2048,128]{1,0:T(8,128)} %x_ref.1, f32[1024,128]{1,0:T(8,128)} %y_ref.1, f32[16,128]{1,0:T(8,128)} %bitcast.4, f32[8,128]{1,0:T(8,128)} %bitcast.6), custom_call_target="tpu_custom_call" | custom-call | flops 6000000000 | bytes 4194304 | tf_op jit(solution)/shard_map/coupling/pallas_call | solution.py:377
  101.4 2.0 %deliver.1 = (f32[16,128]{1,0:T(8,128)}, f32[8,128]{1,0:T(8,128)}, f32[2048,128]{1,0:T(8,128)}) custom-call(f32[16,128]{1,0:T(8,128)} %get-tuple-element.9.sp_in, f32[8,128]{1,0:T(8,128)} %get-tuple-element.10.tp_in, f32[2048,128]{1,0:T(8,128)} %get-tuple-element.11.bary_in), custom_call_target="tpu_custom_call" | custom-call | tf_op jit(solution)/shard_map/deliver/pallas_call | solution.py:433

commit v9 on v8

--- a/solution.py
+++ b/solution.py
@@ -20,7 +20,7 @@
 ROWS, COLS = 2048, 1024
 RCH, CCH = ROWS // LANES, COLS // LANES
 OWN = ROWS // NTGT
-O_CHUNKS = 2
+O_CHUNKS = 4
 MATES = GRID_X * 2
 DELIVERIES = 4
 PIECE = COLS // MATES
@@ -220,6 +220,7 @@
 
         rs[it, t] = l_row[it]
         if it == 0:
+            t_step(2)
             for k in range(RCH):
                 turned = x_ref[k * LANES : (k + 1) * LANES, :].T
                 nx[k : k + 1, :] = jnp.sum(turned * turned, axis=0, keepdims=True)
@@ -233,6 +234,8 @@
         wait_bytes(rs.at[it, pl.ds(0, NTGT - 1)], rs_sem.at[it, 1])
         row_pot = LOG2E * la_ref[...] - combine(rs[it])
         pv[...] = row_pot
+        if it == 0:
+            t_step(4)
         lse_across(zt, pv, tops, totals, l_col.at[it])
 
         @pl.loop(1, NSRC)
@@ -241,10 +244,9 @@
 
         cr[it, s] = l_col[it]
         if it == 0:
-            t_step(2)
             wait_bytes(xs.at[pl.ds(0, MATES - 1)], xs_sem.at[1])
             last_rows(0, MATES)
-            t_step(4)
+            t_step(6)
         else:
             sp_ref[...] = row_pot * LN2 + nx[...]
             last_scores(NTGT // 4, NTGT // 2)
@@ -254,7 +256,6 @@
         if it == 0:
             for k in range(CCH):
                 qb[k * LANES : (k + 1) * LANES, :] = spread(q[k : k + 1, :])
-            t_step(6)
 
     for k in range(CCH):
         qs[k] = q[k : k + 1, :]

time: 104 us -> 103 us (level)
  Pallas kernels: 103 us -> 101 us
    pallas_call x1, Pallas kernels: 101 us -> 98.8 us  [on_device(): pl.pallas_call(kernel, out_shape=(jax.ShapeDtypeStruct((RCH, LANES), F32)...]
where the time goes in v9:
time: 103 us; the launch traced here: 102 us
  Pallas kernels  101 us (98%)
    pallas_call x1, Pallas kernels, on_device(): pl.pallas_call(kernel, out_shape=(jax.ShapeDtypeStruct((RCH, LANES), F32)...  98.8 us

profile of v9, /device:TPU:6, one launch (start us, length us, event | category | flops | bytes accessed | tf_op | source)
XLA Modules:
  0.0 101.5 jit_solution(15189050687905827796)
XLA Ops:
  0.6 98.8 %coupling.1 = (f32[16,128]{1,0:T(8,128)}, f32[8,128]{1,0:T(8,128)}, f32[2048,128]{1,0:T(8,128)}) custom-call(f32[2048,128]{1,0:T(8,128)} %x_ref.1, f32[1024,128]{1,0:T(8,128)} %y_ref.1, f32[16,128]{1,0:T(8,128)} %bitcast.4, f32[8,128]{1,0:T(8,128)} %bitcast.6), custom_call_target="tpu_custom_call" | custom-call | flops 6000000000 | bytes 4194304 | tf_op jit(solution)/shard_map/coupling/pallas_call | solution.py:378
  99.5 2.0 %deliver.1 = (f32[16,128]{1,0:T(8,128)}, f32[8,128]{1,0:T(8,128)}, f32[2048,128]{1,0:T(8,128)}) custom-call(f32[16,128]{1,0:T(8,128)} %get-tuple-element.9.sp_in, f32[8,128]{1,0:T(8,128)} %get-tuple-element.10.tp_in, f32[2048,128]{1,0:T(8,128)} %get-tuple-element.11.bary_in), custom_call_target="tpu_custom_call" | custom-call | tf_op jit(solution)/shard_map/deliver/pallas_call | solution.py:434

commit v10 on v9

--- a/solution.py
+++ b/solution.py
@@ -20,7 +20,7 @@
 ROWS, COLS = 2048, 1024
 RCH, CCH = ROWS // LANES, COLS // LANES
 OWN = ROWS // NTGT
-O_CHUNKS = 4
+O_CHUNKS = 2
 MATES = GRID_X * 2
 DELIVERIES = 4
 PIECE = COLS // MATES
@@ -98,7 +98,7 @@
 def kernel(
     x_ref, y_ref, la_ref, lb_ref, sp_ref, tp_ref, out_ref,
     xt, ya, zt, zf, qb, pv, nx, ny, top8, total8, tops, totals,
-    l_row, rs, l_col, cr, qs, qg, tg, xs, xf, yf, mf, sf, acc, part, shares,
+    l_row, rs, l_col, cr, qs, qg, tg, xs, xf, yf, mf, sf, wh, wl, part, shares,
     rs_sem, cr_sem, qg_sem, tr_send, tr_recv, or_send, or_recv, xs_sem, part_sem,
 ):
     s, t = lax.axis_index("src"), lax.axis_index("tgt")
@@ -276,38 +276,27 @@
         @pl.loop(0, 2 * OWN // depth)
         def _(r):
             at = pl.ds(pl.multiple_of(base + r * depth, depth), depth)
-            best = zf[at, 0:LANES] + qg[0]
-            for b in range(1, NTGT):
-                best = jnp.maximum(best, zf[at, b * LANES : (b + 1) * LANES] + qg[b])
             to = pl.ds(pl.multiple_of(r * depth, depth), depth)
-            mf[to, :] = jnp.broadcast_to(jnp.max(best, axis=1, keepdims=True), (depth, LANES))
-
-        sf[...] = jnp.zeros_like(sf)
-        acc[...] = jnp.zeros_like(acc)
-        at = pl.ds(pl.multiple_of(base, 2 * OWN), 2 * OWN)
-        group = 4
-
-        @pl.loop(0, NTGT // group, unroll=2)
-        def _(b):
-            highs, lows = [], []
-            total = sf[...]
-            for k in range(group):
-                lane = pl.ds(pl.multiple_of((b * group + k) * LANES, LANES), LANES)
-                w = jnp.exp2(zf[at, lane] + qg[b * group + k] - mf[...])
+            lanes = [slice(b * LANES, (b + 1) * LANES) for b in range(NTGT)]
+            best = functools.reduce(jnp.maximum, [zf[at, lanes[b]] + qg[b] for b in range(NTGT)])
+            best = jnp.broadcast_to(jnp.max(best, axis=1, keepdims=True), (depth, LANES))
+            total = jnp.zeros((depth, LANES), F32)
+            for b in range(NTGT):
+                w = jnp.exp2(zf[at, lanes[b]] + qg[b] - best)
                 total += w
                 high = w.astype(BF16)
-                highs.append(high)
-                lows.append((w - high.astype(F32)).astype(BF16))
-            sf[...] = total
-            ys = pl.ds(pl.multiple_of(b * group * LANES, group * LANES), group * LANES)
-            both = jnp.dot(jnp.concatenate(highs, axis=1), yf[ys, 0 : 2 * LATENT], preferred_element_type=F32)
-            rest = jnp.dot(jnp.concatenate(lows, axis=1), yf[ys, 0:LATENT], preferred_element_type=F32)
-            acc[...] += both[:, :LATENT] + both[:, LATENT:] + rest
+                wh[to, lanes[b]] = high
+                wl[to, lanes[b]] = (w - high.astype(F32)).astype(BF16)
+            mf[to, :] = best
+            sf[to, :] = total
+
+        both = dot(wh[...], yf[...])
+        sums = both[:, :LATENT] + both[:, LATENT:] + dot(wl[...], yf[:, 0:LATENT])
 
         for g in range(2):
             rows = slice(g * OWN, (g + 1) * OWN)
             to = chip * 2 + g
-            part[to, 0:OWN, :] = acc[rows, :]
+            part[to, 0:OWN, :] = sums[rows, :]
             part[to, OWN : OWN + 1, :] = mf[rows, :].T[0:1, :]
             part[to, OWN + 1 : OWN + 2, :] = jnp.sum(sf[rows, :].T, axis=0, keepdims=True)
 
@@ -409,7 +398,8 @@
             pltpu.VMEM((NTGT * PIECE, 2 * LATENT), BF16),
             pltpu.VMEM((2 * OWN, LANES), F32),
             pltpu.VMEM((2 * OWN, LANES), F32),
-            pltpu.VMEM((2 * OWN, LATENT), F32),
+            pltpu.VMEM((2 * OWN, NTGT * PIECE), BF16),
+            pltpu.VMEM((2 * OWN, NTGT * PIECE), BF16),
             pltpu.VMEM((MATES, OWN + 8, LATENT), F32),
             pltpu.VMEM((MATES, OWN + 8, LATENT), F32),
             dma((ITERS, 2)),

time: 103 us -> 103 us (level)
  no operation moved by 1% of the time
where the time goes in v10:
time: 103 us; the launch traced here: 102 us
  Pallas kernels  101 us (98%)
    pallas_call x1, Pallas kernels, on_device(): pl.pallas_call(kernel, out_shape=(jax.ShapeDtypeStruct((RCH, LANES), F32)...  99 us

profile of v10, /device:TPU:6, one launch (start us, length us, event | category | flops | bytes accessed | tf_op | source)
XLA Modules:
  0.0 101.7 jit_solution(10875036636833727196)
XLA Ops:
  0.6 99.0 %coupling.1 = (f32[16,128]{1,0:T(8,128)}, f32[8,128]{1,0:T(8,128)}, f32[2048,128]{1,0:T(8,128)}) custom-call(f32[2048,128]{1,0:T(8,128)} %x_ref.1, f32[1024,128]{1,0:T(8,128)} %y_ref.1, f32[16,128]{1,0:T(8,128)} %bitcast.4, f32[8,128]{1,0:T(8,128)} %bitcast.6), custom_call_target="tpu_custom_call" | custom-call | flops 6000000000 | bytes 4194304 | tf_op jit(solution)/shard_map/coupling/pallas_call | solution.py:367
  99.6 2.0 %deliver.1 = (f32[16,128]{1,0:T(8,128)}, f32[8,128]{1,0:T(8,128)}, f32[2048,128]{1,0:T(8,128)}) custom-call(f32[16,128]{1,0:T(8,128)} %get-tuple-element.9.sp_in, f32[8,128]{1,0:T(8,128)} %get-tuple-element.10.tp_in, f32[2048,128]{1,0:T(8,128)} %get-tuple-element.11.bary_in), custom_call_target="tpu_custom_call" | custom-call | tf_op jit(solution)/shard_map/deliver/pallas_call | solution.py:424
